TPU v7x, 256 devices: a whole 4x4x8 slice. The times are simulated.
256 devices in a mesh: ctx: 64 (over y, z, core), head: 4 (over x).
Axes of the slice: x: 4, y: 4, z: 8, core: 2. Of those that a mesh axis runs over, the one named last changes fastest.
Arguments:
- tokens_in: bfloat16 [8192, 12288], P('ctx'), may hold values from -16 to 16
- w_key: bfloat16 [12288, 512], P('ctx', 'head'), may hold values from -0.0546875 to 0.0546875
- w_value: bfloat16 [12288, 512], P('ctx', 'head'), may hold values from -0.0546875 to 0.0546875
- queries: bfloat16 [8192, 6144], P('ctx', 'head'), may hold values from -140 to 140
- out_grad: bfloat16 [8192, 6144], P('ctx', 'head'), may hold values from -24 to 24
- attn_out: bfloat16 [8192, 6144], P('ctx', 'head'), may hold values from -6 to 6
- doc_ids: int32 [8192], P('ctx'), may hold values from 0 to 2, never falling along the last dimension, each value on 1 to 6144 neighbouring positions
Outputs:
- grad_wk: float32 [12288, 512], P('ctx', 'head')
- grad_wv: float32 [12288, 512], P('ctx', 'head')
- input_grad: float32 [8192, 12288], P('ctx', 'head')
All inputs are finite; a program needn't handle non-finite values.
Results may differ from a plain program's by a relative error of at most 0.017.
Values may be sent and summed in bfloat16 or wider, within the bound.
No kernel may reach another device: no remote copies, remote signals or barrier semaphores. Data moves between devices by JAX's collectives and lax.ppermute only.
A program may use at most 128 MiB of HBM per device.

v0:
```python
import math

import jax
import jax.numpy as jnp
from jax import lax
from jax.sharding import PartitionSpec as P

HD = 128
WINDOW = 4096


def body(tokens_in, w_key, w_value, queries, out_grad, attn_out, doc_ids):
    rows = tokens_in.shape[0]
    head_size = w_key.shape[1]
    heads = queries.shape[1] // HD
    scale = 1.0 / math.sqrt(HD)
    count = lax.axis_size("ctx")
    place = lax.axis_index("ctx")
    need = min(WINDOW // rows + 1, count)
    span = need * rows
    seg_all = lax.all_gather(doc_ids, "ctx", axis=0, tiled=True)
    both = jnp.concatenate((w_key, w_value), 1)
    full_weights = lax.all_gather(both, "ctx", axis=0, tiled=True)
    kv_float = jnp.dot(tokens_in, full_weights, preferred_element_type=jnp.float32)
    kv_local = kv_float.astype(jnp.bfloat16)
    whole = lax.all_gather(kv_local, "ctx", axis=0, tiled=True)
    padded = jnp.concatenate(
        (jnp.zeros(((need - 1) * rows, 2 * head_size), jnp.bfloat16), whole), 0
    )
    band = lax.dynamic_slice_in_dim(padded, place * rows, span, 0)
    seg_pad = jnp.concatenate((jnp.full(((need - 1) * rows,), -1, jnp.int32), seg_all), 0)
    key_seg = lax.dynamic_slice_in_dim(seg_pad, place * rows, span, 0)
    key_pos = (place - need + 1) * rows + jnp.arange(span, dtype=jnp.int32)
    query_pos = place * rows + jnp.arange(rows, dtype=jnp.int32)
    visible = (key_pos[None, :] <= query_pos[:, None]) & (
        query_pos[:, None] - key_pos[None, :] < WINDOW
    )
    visible = visible & (key_pos[None, :] >= 0) & (key_seg[None, :] == doc_ids[:, None])
    keys = band[:, :head_size]
    values = band[:, head_size:]
    delta = jnp.sum(
        out_grad.astype(jnp.float32).reshape(rows, heads, HD)
        * attn_out.astype(jnp.float32).reshape(rows, heads, HD),
        -1,
    )
    query_groups = jnp.moveaxis(queries.reshape(rows, heads // 4, 4, HD), 1, 0)
    grad_groups = jnp.moveaxis(out_grad.reshape(rows, heads // 4, 4, HD), 1, 0)
    delta_groups = jnp.moveaxis(delta.reshape(rows, heads // 4, 4), 1, 0)

    def attend(carry, items):
        dk_acc, dv_acc = carry
        q_block, o_block, d_block = items
        scores = (
            jnp.einsum("tjd,kd->jtk", q_block, keys, preferred_element_type=jnp.float32) * scale
        )
        scores = jnp.where(visible[None], scores, -jnp.inf)
        top = jnp.max(scores, -1, keepdims=True)
        weights = jnp.exp(scores - top)
        weights = weights / jnp.sum(weights, -1, keepdims=True)
        rounded = weights.astype(jnp.bfloat16)
        dv_acc = dv_acc + jnp.einsum(
            "jtk,tjd->kd", rounded, o_block, preferred_element_type=jnp.float32
        )
        dp = jnp.einsum("tjd,kd->jtk", o_block, values, preferred_element_type=jnp.float32)
        ds = (weights * (dp - d_block.T[:, :, None])).astype(jnp.bfloat16)
        dk_acc = (
            dk_acc
            + jnp.einsum("jtk,tjd->kd", ds, q_block, preferred_element_type=jnp.float32) * scale
        )
        return ((dk_acc, dv_acc), None)

    empty = jnp.zeros((span, head_size), jnp.float32)
    (dk_band, dv_band), _ = lax.scan(
        attend, (empty, empty), (query_groups, grad_groups, delta_groups)
    )
    partials = jnp.concatenate((dk_band, dv_band), 1)
    spread = jnp.zeros(((count + need - 1) * rows, 2 * head_size), jnp.float32)
    spread = lax.dynamic_update_slice_in_dim(spread, partials, place * rows, 0)
    owned = lax.psum_scatter(spread[(need - 1) * rows :], "ctx", scatter_dimension=0, tiled=True)
    grad_terms = owned.astype(jnp.bfloat16)
    contract = (((0,), (0,)), ((), ()))
    grads = lax.psum_scatter(
        lax.dot_general(tokens_in, grad_terms, contract, preferred_element_type=jnp.float32),
        "ctx",
        scatter_dimension=0,
        tiled=True,
    )
    across = (((1,), (1,)), ((), ()))
    term = lax.dot_general(grad_terms, full_weights, across, preferred_element_type=jnp.float32)
    input_grad = lax.psum_scatter(
        term.astype(jnp.bfloat16), "head", scatter_dimension=1, tiled=True
    ).astype(jnp.float32)
    return (grads[:, :head_size], grads[:, head_size:], input_grad)


def solution(mesh):
    return jax.shard_map(
        body,
        mesh=mesh,
        in_specs=(
            P("ctx", None),
            P("ctx", "head"),
            P("ctx", "head"),
            P("ctx", "head"),
            P("ctx", "head"),
            P("ctx", "head"),
            P("ctx"),
        ),
        out_specs=(P("ctx", "head"), P("ctx", "head"), P("ctx", "head")),
        check_vma=False,
    )
```

profile of v0, /device:TPU:1, one launch (start us, length us, event | category | flops | bytes accessed | tf_op | source)
XLA Modules:
  0.0 631.6 jit_solution(8519254877434610808)
XLA Ops:
  7.2 0.0 copy-start
  7.2 0.0 all-gather.4.cloned.1.call-start
  7.2 1.6 pad_maximum_fusion
  8.9 0.0 all-gather.4.cloned.1.call-update
  8.9 0.0 copy-start.4
  8.9 0.0 all-gather.6.cloned.1.call-start
  8.9 87.8 %all-gather.4.cloned.1.call-done = bf16[12288,256]{1,0:T(8,128)(2,1)} async-done(((bf16[192,256]{1,0:T(8,128)(2,1)}), bf16[12288,256]{1,0:T(8,128)(2,1)}) %all-gather.4.cloned.1.call-update) | async-done | bytes 6291472 | tf_op jit(solution)/shard_map/all_gather | solution.py:23
  96.7 0.0 copy-done
  96.7 5.3 fusion.34
  102.0 0.0 all-gather.6.cloned.1.call-update
  102.0 0.0 reduce-scatter.6.cloned.1.call-start
  102.1 0.0 copy-done.4
  102.1 0.9 copy.31
  103.0 1.2 copy.30
  104.2 1.9 copy.33
  106.2 2.1 convert_multiply_fusion
  108.2 1.2 reduce_sum.18
  109.4 0.6 reshape.38
  110.0 38.1 %all-gather = s32[64,1,128]{2,1,0:T(1,128)S(1)} all-gather(s32[1,1,128]{2,1,0:T(1,128)} %bitcast.7), channel_id=1, replica_groups=mesh['ctx'=64,'head'=4] {'ctx'}, dimensions={0}, use_global_device_ids=true | all-gather | bytes 33280 | tf_op jit(solution)/shard_map/all_gather | solution.py:21
  148.1 0.6 iota_add_fusion.1
  148.7 0.6 iota_add_fusion
  149.3 0.7 pad_dynamic-slice_fusion.2
  150.0 25.1 %all-gather.6.cloned.1.call-done = bf16[8192,256]{0,1:T(8,128)(2,1)} async-done(((bf16[128,256]{0,1:T(8,128)(2,1)}), bf16[8192,256]{0,1:T(8,128)(2,1)}) %all-gather.6.cloned.1.call-update) | async-done | bytes 4194320 | tf_op jit(solution)/shard_map/all_gather | solution.py:26
  175.1 2.5 pad_dynamic-slice_fusion.1
  177.6 2.3 copy.37
  180.0 2.3 copy.35
  182.3 75.9 %while.13 = (s32[]{:T(128)}, f32[4224,128]{1,0:T(8,128)}, f32[4224,128]{1,0:T(8,128)}, bf16[3,128,4,128]{1,3,2,0:T(8,128)(2,1)S(1)}, bf16[4224,128]{1,0:T(8,128)...) while((s32[]{:T(128)}, f32[4224,128]{1,0:T(8,128)}, ...), condition=%wide.region_4.5_spmd.clone, body=%wide.region_1.4_spmd.clone.sunk | while | flops 2242711552 | bytes 55725864 | solution.py:73
  182.3 0.7 dynamic-slice_bitcast_fusion.2
  183.0 1.6 fusion.61
  184.6 2.6 multiply_select_fusion.2
  187.2 4.8 fusion.62
  192.0 8.5 %fusion.63 = f32[4224,128]{1,0:T(8,128)} fusion(f32[4224,128]{1,0:T(8,128)} %get-tuple-element.281, f32[4,128]{1,0:T(4,128)S(1)} %dynamic-slice_bitcast_fusion.2, f32[4,128,4224]{2,1,0:T(8,128)} %get-tuple-element.263, f32[4,128]{1,0:T(4,128)S(1)} %get-tuple-element.264, bf16[4224,128]{1,0:T(8,128)(2,1)} %get-tuple-element.301, pred[]{:T(512)S(6)} %compare.5, ...), kind=kOutput, calls=%fused_computation.13.clone.1 | convolution fusion | flops 1117569024 | bytes 14325248 | tf_op jit(solution)/shard_map/while/body/eval_jaxpr/jtk,tjd->kd/dot_general | solution.py:68
  200.5 6.3 fusion.64
  206.8 0.7 dynamic-slice_bitcast_fusion.2
  207.4 1.6 fusion.61
  209.0 2.6 multiply_select_fusion.2
  211.7 4.8 fusion.62
  216.5 9.1 %fusion.63 = f32[4224,128]{1,0:T(8,128)} fusion(f32[4224,128]{1,0:T(8,128)} %get-tuple-element.281, f32[4,128]{1,0:T(4,128)S(1)} %dynamic-slice_bitcast_fusion.2, f32[4,128,4224]{2,1,0:T(8,128)} %get-tuple-element.263, f32[4,128]{1,0:T(4,128)S(1)} %get-tuple-element.264, bf16[4224,128]{1,0:T(8,128)(2,1)} %get-tuple-element.301, pred[]{:T(512)S(6)} %compare.5, ...), kind=kOutput, calls=%fused_computation.13.clone.1 | convolution fusion | flops 1117569024 | bytes 14325248 | tf_op jit(solution)/shard_map/while/body/eval_jaxpr/jtk,tjd->kd/dot_general | solution.py:68
  225.6 6.9 %fusion.64 = f32[4224,128]{1,0:T(8,128)} fusion(f32[4,128,4224]{2,1,0:T(8,128)} %get-tuple-element.263, f32[4,128]{1,0:T(4,128)S(1)} %get-tuple-element.264, f32[4224,128]{1,0:T(8,128)} %get-tuple-element.282, pred[]{:T(512)S(6)} %compare.5, bf16[3,128,4,128]{1,3,2,0:T(8,128)(2,1)} %get-tuple-element.300, s32[]{:T(128)S(6)} %copy.51), kind=kOutput, calls=%fused_computation.14.clone.1 | convolution fusion | flops 559054848 | bytes 13109253 | tf_op jit(solution)/shard_map/while/body/eval_jaxpr/jtk,tjd->kd/dot_general | solution.py:61
  232.5 0.7 dynamic-slice_bitcast_fusion.2
  233.2 1.6 fusion.61
  234.8 2.6 multiply_select_fusion.2
  237.4 4.8 fusion.62
  242.2 9.1 %fusion.63 = f32[4224,128]{1,0:T(8,128)} fusion(f32[4224,128]{1,0:T(8,128)} %get-tuple-element.281, f32[4,128]{1,0:T(4,128)S(1)} %dynamic-slice_bitcast_fusion.2, f32[4,128,4224]{2,1,0:T(8,128)} %get-tuple-element.263, f32[4,128]{1,0:T(4,128)S(1)} %get-tuple-element.264, bf16[4224,128]{1,0:T(8,128)(2,1)} %get-tuple-element.301, pred[]{:T(512)S(6)} %compare.5, ...), kind=kOutput, calls=%fused_computation.13.clone.1 | convolution fusion | flops 1117569024 | bytes 14325248 | tf_op jit(solution)/shard_map/while/body/eval_jaxpr/jtk,tjd->kd/dot_general | solution.py:68
  251.3 6.9 %fusion.64 = f32[4224,128]{1,0:T(8,128)} fusion(f32[4,128,4224]{2,1,0:T(8,128)} %get-tuple-element.263, f32[4,128]{1,0:T(4,128)S(1)} %get-tuple-element.264, f32[4224,128]{1,0:T(8,128)} %get-tuple-element.282, pred[]{:T(512)S(6)} %compare.5, bf16[3,128,4,128]{1,3,2,0:T(8,128)(2,1)} %get-tuple-element.300, s32[]{:T(128)S(6)} %copy.51), kind=kOutput, calls=%fused_computation.14.clone.1 | convolution fusion | flops 559054848 | bytes 13109253 | tf_op jit(solution)/shard_map/while/body/eval_jaxpr/jtk,tjd->kd/dot_general | solution.py:61
  258.2 0.8 broadcast_in_dim.12
  259.1 0.8 copy-done.1
  259.8 0.7 copy-done.2
  260.5 0.6 maximum_dynamic-update-slice_fusion
  261.1 3.8 slice.20
  264.8 0.0 reduce-scatter.6.cloned.1.call-update
  264.8 0.3 reduce-scatter.8.cloned.1.call-start
  265.1 145.9 %reduce-scatter.6.cloned.1.call-done = f32[128,256]{1,0:T(8,128)} async-done(((f32[8192,256]{1,0:T(8,128)}), f32[128,256]{1,0:T(8,128)}) %reduce-scatter.6.cloned.1.call-update) | async-done | bytes 131088 | tf_op jit(solution)/shard_map/reduce_scatter | solution.py:79
  411.0 6.8 %convolution_convert_fusion = bf16[128,12288]{1,0:T(8,128)(2,1)} fusion(bf16[12288,256]{1,0:T(8,128)(2,1)} %all-gather.4.cloned.1.call-done, f32[128,256]{1,0:T(8,128)} %reduce-scatter.6.cloned.1.call-done), kind=kOutput, calls=%fused_computation.36 | convolution fusion | flops 806912000 | bytes 9568256 | tf_op jit(solution)/shard_map/dot_general | solution.py:89
  417.8 0.0 reduce-scatter.8.cloned.1.call-update
  417.8 0.0 reduce-scatter.10.cloned.1.call-start
  417.9 0.8 copy-done.3
  418.7 6.3 convolution_bitcast_fusion.2
  425.0 12.6 %copy.42 = f32[12288,256]{1,0:T(8,128)} copy(f32[12288,256]{0,1:T(8,128)} %convolution_bitcast_fusion.2) | data formatting | bytes 25165824
  437.6 0.0 reduce-scatter.10.cloned.1.call-update
  437.7 24.4 %reduce-scatter.8.cloned.1.call-done = bf16[128,3072]{1,0:T(8,128)(2,1)} async-done(((bf16[128,12288]{1,0:T(8,128)(2,1)}), bf16[128,3072]{1,0:T(8,128)(2,1)}) %reduce-scatter.8.cloned.1.call-update) | async-done | bytes 786448 | tf_op jit(solution)/shard_map/reduce_scatter | solution.py:90
  462.1 2.4 convert_element_type.33
  464.5 158.9 %reduce-scatter.10.cloned.1.call-done = f32[192,256]{1,0:T(8,128)} async-done(((f32[12288,256]{1,0:T(8,128)}), f32[192,256]{1,0:T(8,128)}) %reduce-scatter.10.cloned.1.call-update) | async-done | bytes 196624
  623.5 1.6 fusion.38
  (6 shorter events, 0.0 us)
Async XLA Ops:
  7.2 89.6 %copy-start = (bf16[128,12288]{1,0:T(8,128)(2,1)S(1)}, bf16[128,12288]{1,0:T(8,128)(2,1)}, u32[]{:S(2)}) copy-start(bf16[128,12288]{1,0:T(8,128)(2,1)} %param.9) | copy-start | bytes 9437188
  7.2 89.6 %all-gather.4.cloned.1.call-start = ((), (), s32[]{:S(2)}) async-start(), calls=%async_computation.3 | async-start | bytes 6389760 | tf_op jit(solution)/shard_map/all_gather | solution.py:23
  8.9 93.2 %copy-start.4 = (bf16[128,1536]{1,0:T(8,128)(2,1)S(1)}, bf16[128,1536]{1,0:T(8,128)(2,1)}, u32[]{:S(2)}) copy-start(bf16[128,1536]{1,0:T(8,128)(2,1)} %param.13) | copy-start | bytes 1179652
  8.9 166.2 %all-gather.6.cloned.1.call-start = ((), (), s32[]{:S(2)}) async-start(), calls=%async_computation.4 | async-start | bytes 4259840 | tf_op jit(solution)/shard_map/all_gather | solution.py:26
  102.0 309.0 %reduce-scatter.6.cloned.1.call-start = ((), (), s32[]{:S(2)}) async-start(), calls=%async_computation.5 | async-start | bytes 8519680 | tf_op jit(solution)/shard_map/reduce_scatter | solution.py:79
  258.2 1.6 copy-start.1
  258.2 2.3 copy-start.2
  264.8 197.3 %reduce-scatter.8.cloned.1.call-start = ((), (), s32[]{:S(2)}) async-start(), calls=%async_computation.6 | async-start | bytes 3932160 | tf_op jit(solution)/shard_map/reduce_scatter | solution.py:90
  417.8 0.9 copy-start.3
  417.8 205.6 %reduce-scatter.10.cloned.1.call-start = ((), (), s32[]{:S(2)}) async-start(), calls=%async_computation.7 | async-start | bytes 12779520
Sparse Core Ops, SparseCore 0:
  11.3 85.3 all-gather.3
  102.1 72.8 all-gather.5
  265.0 146.0 reduce-scatter.5
  417.9 44.1 reduce-scatter.7
  466.8 156.5 reduce-scatter.9
where the time goes:
time: 636 us; the launch traced here: 632 us
  waiting for transfers between devices  442 us (69%)
  matrix products  72.9 us (11%)
  blocking collectives  38.1 us (6%)
  local copies, waits for them, and re-layouts  35.7 us (6%)
  other arithmetic  28.3 us (4%)
  between operations  13.9 us (2%)
    unnamed x6, waiting for transfers between devices  159 us
    reduce_scatter x1, waiting for transfers between devices, body(): lax.psum_scatter(spread[(need - 1) * rows:], 'ctx', scatter_dimension=0,...  146 us
    all_gather x1, waiting for transfers between devices, body(): full_weights = lax.all_gather(both, 'ctx', axis=0, tiled=True)  87.8 us
    all_gather x1, blocking collectives, body(): seg_all = lax.all_gather(doc_ids, 'ctx', axis=0, tiled=True)  38.1 us
    dot_general x3, matrix products, attend(): jnp.einsum('jtk,tjd->kd', ds, q_block, preferred_element_type=jnp.float32)  26.7 us
    all_gather x1, waiting for transfers between devices, body(): whole = lax.all_gather(kv_local, 'ctx', axis=0, tiled=True)  25.1 us
    reduce_scatter x1, waiting for transfers between devices, body(): lax.psum_scatter(term.astype(jnp.bfloat16), 'head', scatter_dimension=1,...  24.4 us
    unnamed x16, local copies, waits for them, and re-layouts  23.6 us
  transfers between devices with their start and end apart: 5, of which 5 were waited for; matrix products, arithmetic and copies ran while one was open for 5% of the time, Pallas kernels for 0%

commit v1 on v0

v1 whole, which is shorter than its diff:
```python
import math

import jax
import jax.numpy as jnp
from jax import lax
from jax.experimental import pallas as pl
from jax.experimental.pallas import tpu as pltpu
from jax.sharding import Mesh
from jax.sharding import PartitionSpec as P

HD = 128
WINDOW = 4096
ROWS = 128
PAIR = 2 * ROWS
RING = 8
PLANE = RING * ROWS
CHUNKS = WINDOW // PAIR + 1
SPAN = CHUNKS * PAIR
GROUP = 4
TILE = GROUP * ROWS
SCALE = 1.0 / math.sqrt(HD)
RATE = SCALE * math.log2(math.e)
HIDDEN = -1e30

NT = (((1,), (1,)), ((), ()))
NN = (((1,), (0,)), ((), ()))
TN = (((0,), (0,)), ((), ()))


def dot(a, b, dims):
    return lax.dot_general(a, b, dims, preferred_element_type=jnp.float32)


def attend(
    place, own0, own1, own2, far0, far1, far2, q_ref, o_ref, delta_ref, doc_ref,
    near_out, far_out, k_s, v_s, p_s, m_s, dk_s, dv_s,
):
    z = place[0]
    c = place[1]
    odd = place[2]
    planes = ((own0, far0), (own1, far1), (own2, far2))
    for plane, pair in enumerate(planes):

        @pl.loop(0, RING)
        def load(step, plane=plane, pair=pair):
            j = plane * RING + step + odd * (1 - 2 * (step % 2)) - z

            @pl.when((j >= 0) & (j < CHUNKS))
            def _():
                for slot, ref in enumerate(pair):
                    core = c if slot == 0 else 1 - c
                    src = pl.ds(pl.multiple_of(step * ROWS, ROWS), ROWS)
                    dst = pl.ds(pl.multiple_of(j * PAIR + core * ROWS, ROWS), ROWS)
                    k_s[dst, :] = ref[src, :HD]
                    v_s[dst, :] = ref[src, HD:]

    doc = doc_ref[...]
    token = c * ROWS + lax.broadcasted_iota(jnp.int32, (1, TILE), 1) % ROWS
    high = token + WINDOW
    start = jnp.where(doc == 0, place[3], jnp.where(doc == 1, place[4], place[5]))
    low = jnp.maximum(start, token + 1)
    row = lax.broadcasted_iota(jnp.int32, (PAIR, TILE), 0)

    for g in range(q_ref.shape[0] // TILE):
        q = q_ref[g * TILE : (g + 1) * TILE, :]
        o = o_ref[g * TILE : (g + 1) * TILE, :]
        delta = delta_ref[g]

        def first(j, carry, q=q):
            top, total = carry
            at = pl.ds(pl.multiple_of(j * PAIR, PAIR), PAIR)
            s = dot(k_s[at, :], q, NT)
            seen = (row >= low - j * PAIR) & (row <= high - j * PAIR)
            s = jnp.where(seen, s, HIDDEN)
            peak = jnp.maximum(top, jnp.max(s, 0, keepdims=True))
            p = jnp.exp2((s - peak) * RATE)
            p_s[at, :] = p
            m_s[j] = peak
            total = total * jnp.exp2((top - peak) * RATE) + jnp.sum(p, 0, keepdims=True)
            return peak, total

        top, total = lax.fori_loop(
            0,
            CHUNKS,
            first,
            (jnp.full((1, TILE), HIDDEN, jnp.float32), jnp.zeros((1, TILE), jnp.float32)),
        )
        share = 1.0 / total

        def second(j, carry, g=g, q=q, o=o, delta=delta, top=top, share=share):
            at = pl.ds(pl.multiple_of(j * PAIR, PAIR), PAIR)
            p = p_s[at, :] * (jnp.exp2((m_s[j] - top) * RATE) * share)
            dp = dot(v_s[at, :], o, NT)
            ds = (p * (dp - delta)).astype(jnp.bfloat16)
            dv = dot(p.astype(jnp.bfloat16), o, NN)
            dk = dot(ds, q, NN)
            if g == 0:
                dv_s[at, :] = dv
                dk_s[at, :] = dk
            else:
                dv_s[at, :] += dv
                dk_s[at, :] += dk
            return carry

        lax.fori_loop(0, CHUNKS, second, 0)

    for plane in range(3):

        @pl.loop(0, RING)
        def store(step, plane=plane):
            j = plane * RING + step + odd * (1 - 2 * (step % 2)) - z
            block = plane * RING + step + odd * (1 - 2 * (step % 2))
            dst = pl.ds(pl.multiple_of(block * ROWS, ROWS), ROWS)
            inside = (j >= 0) & (j < CHUNKS)

            @pl.when(inside)
            def _():
                for slot, ref in enumerate((near_out, far_out)):
                    core = c if slot == 0 else 1 - c
                    src = pl.ds(pl.multiple_of(j * PAIR + core * ROWS, ROWS), ROWS)
                    ref[dst, :HD] = (dk_s[src, :] * SCALE).astype(jnp.bfloat16)
                    ref[dst, HD:] = dv_s[src, :].astype(jnp.bfloat16)

            @pl.when(jnp.logical_not(inside))
            def _():
                for ref in (near_out, far_out):
                    ref[dst, :] = jnp.zeros((ROWS, 2 * HD), jnp.bfloat16)


def attention(place, kv, q, o, delta, doc):
    out = jax.ShapeDtypeStruct((3 * PLANE, 2 * HD), jnp.bfloat16)
    heads = q.shape[0] // ROWS
    vmem = pl.BlockSpec(memory_space=pltpu.VMEM)
    return pl.pallas_call(
        attend,
        out_shape=(out, out),
        in_specs=[pl.BlockSpec(memory_space=pltpu.SMEM)] + [vmem] * 10,
        out_specs=(vmem, vmem),
        scratch_shapes=[
            pltpu.VMEM((SPAN, HD), jnp.bfloat16),
            pltpu.VMEM((SPAN, HD), jnp.bfloat16),
            pltpu.VMEM((SPAN, TILE), jnp.float32),
            pltpu.VMEM((CHUNKS, 1, TILE), jnp.float32),
            pltpu.VMEM((SPAN, HD), jnp.float32),
            pltpu.VMEM((SPAN, HD), jnp.float32),
        ],
        compiler_params=pltpu.CompilerParams(vmem_limit_bytes=48 << 20),
        cost_estimate=pl.CostEstimate(
            flops=8 * heads * ROWS * SPAN * HD,
            bytes_accessed=8 << 20,
            transcendentals=heads * ROWS * SPAN,
        ),
        name="attend",
    )(place, *kv, q, o, delta, doc)


def project(rows_ref, key_ref, value_ref, sent, w_s):
    depth = value_ref.shape[1]
    blocks = value_ref.shape[0]
    counts = jnp.zeros((8, HD), jnp.float32)
    for i in range(blocks):
        w_s[i * depth : (i + 1) * depth, :HD] = key_ref[i, :depth, :]
        w_s[i * depth : (i + 1) * depth, HD:] = value_ref[i]
        counts = counts + key_ref[i, depth:, :].astype(jnp.float32)[:8]
    rows = rows_ref[...].reshape(-1, rows_ref.shape[2])
    places = rows_ref.shape[0]
    sent[:, :ROWS, :] = dot(rows, w_s[...], NN).reshape(places, ROWS, 2 * HD)
    sent[:, ROWS:, :HD] = jnp.broadcast_to(counts[None], (places, 8, HD))
    sent[:, ROWS:, HD:] = jnp.zeros((places, 8, HD), jnp.float32)


def weight_terms(core, rows_ref, terms_ref, near, far):
    c = core[0]
    depth = near.shape[1]
    terms = terms_ref[...]
    for z in range(RING):
        cols = rows_ref[:, :, z * 2 * depth : (z + 1) * 2 * depth]
        block = dot(cols.reshape(-1, 2 * depth), terms, TN)
        lower, upper = block[:depth], block[depth:]
        near[z] = jnp.where(c == 0, lower, upper)
        far[z] = jnp.where(c == 0, upper, lower).astype(jnp.bfloat16)


def input_terms(terms_ref, w_ref, out):
    heads, width = w_ref.shape[:2]
    step = 512
    for n in range(0, width, step):
        total = dot(terms_ref[0], w_ref[0, n : n + step, :], NT)
        for h in range(1, heads):
            total = total + dot(terms_ref[h], w_ref[h, n : n + step, :], NT)
        out[:, n : n + step] = total


def kernel_call(f, out_shape, inputs, scratch=(), flops=0):
    smem, vmem = pl.BlockSpec(memory_space=pltpu.SMEM), pl.BlockSpec(memory_space=pltpu.VMEM)
    return pl.pallas_call(
        f,
        out_shape=out_shape,
        in_specs=[smem if a.ndim == 1 else vmem for a in inputs],
        out_specs=jax.tree.map(lambda _: vmem, out_shape),
        scratch_shapes=scratch,
        compiler_params=pltpu.CompilerParams(vmem_limit_bytes=40 << 20),
        cost_estimate=pl.CostEstimate(flops=flops, bytes_accessed=8 << 20, transcendentals=0),
        name=f.__name__,
    )(*inputs)


def split_columns(a, parts):
    rows, width = a.shape[0], a.shape[1] // parts

    def move(src, dst):
        dst[0] = src[...]

    return pl.pallas_call(
        move,
        grid=(parts,),
        out_shape=jax.ShapeDtypeStruct((parts, rows, width), a.dtype),
        in_specs=[pl.BlockSpec((rows, width), lambda i: (0, i))],
        out_specs=pl.BlockSpec((1, rows, width), lambda i: (i, 0, 0)),
        name="split_columns",
    )(a)


def swap(a, axis="c"):
    return lax.ppermute(a, axis, [(0, 1), (1, 0)])


def body(tokens_in, w_key, w_value, queries, out_grad, attn_out, doc_ids):
    f32, bf16 = jnp.float32, jnp.bfloat16
    heads = queries.shape[1] // HD
    y, zb, za, c = (lax.axis_index(name) for name in ("y", "zb", "za", "c"))
    z = zb * 2 + za
    ys = lax.axis_size("y")
    xs = lax.axis_size("x")
    depth = w_key.shape[0]
    model = tokens_in.shape[1]
    shape = jax.ShapeDtypeStruct
    core = c.astype(jnp.int32)[None]
    place = jnp.stack([z, c, za]).astype(jnp.int32)

    cut = split_columns(tokens_in, ys)
    rows_y = lax.all_to_all(cut, "y", 0, 0)

    turned = lax.ppermute(
        jnp.concatenate((w_key, w_value), 1),
        ("y", "x"),
        [(a * xs + b, b * xs + a) for a in range(ys) for b in range(xs)],
    )

    before = jnp.stack([jnp.sum(doc_ids < 1), jnp.sum(doc_ids < 2)]).astype(f32)
    counts = jnp.zeros((16, HD), f32).at[0, :2].set(before).astype(bf16)
    plane_axes = ("zb", "za", "c")
    key_part = lax.all_gather(jnp.concatenate((w_key, counts), 0), plane_axes, axis=0)
    key_part, tied = lax.optimization_barrier((key_part, w_value))
    value_part = lax.all_gather(tied, plane_axes, axis=0)

    def by_head(a):
        return a.reshape(ROWS, heads, HD).swapaxes(0, 1)

    delta = jnp.sum(
        out_grad.astype(f32).reshape(ROWS, heads, HD)
        * attn_out.astype(f32).reshape(ROWS, heads, HD),
        -1,
    )
    delta = delta.T.reshape(heads // GROUP, 1, TILE)
    doc_tile = jnp.tile(doc_ids, GROUP)[None]
    q_rows = by_head(queries).reshape(heads * ROWS, HD)
    o_rows = by_head(out_grad).reshape(heads * ROWS, HD)

    quarter = model // ys
    sent = kernel_call(
        project,
        shape((ys, ROWS + 8, 2 * HD), f32),
        (rows_y, key_part, value_part),
        [pltpu.VMEM((quarter, 2 * HD), bf16)],
        2 * ys * ROWS * quarter * 2 * HD,
    )
    got = lax.all_to_all(sent, "y", 0, 0)
    kv = jnp.sum(got[:, :ROWS], 0).astype(bf16)
    starts = jnp.sum(got[:, ROWS], 0)

    origin = (y * RING + z - WINDOW // PAIR) * PAIR
    starts = jnp.concatenate((jnp.zeros((1,), jnp.int32), starts[:2].astype(jnp.int32)))
    window = jnp.concatenate((place, starts - origin))

    turned, _ = lax.optimization_barrier((turned, kv))
    w_all = lax.all_gather(turned, ("y", "zb", "za", "c"), axis=0, tiled=True)
    w_all = w_all.reshape(xs, quarter, 2 * HD)

    pair = jnp.concatenate((kv, swap(kv, "za")), 0)
    own2 = lax.all_gather(pair, "zb", axis=0, tiled=True)
    own1 = lax.ppermute(own2, "y", [(i, i + 1) for i in range(ys - 1)])
    own0 = lax.ppermute(own2, "y", [(i, i + 2) for i in range(ys - 2)])
    far2, far1, far0 = swap(own2), swap(own1), swap(own0)

    near, far = attention(
        window, (own0, own1, own2, far0, far1, far2), q_rows, o_rows, delta, doc_tile
    )

    mine = near.astype(f32) + swap(far).astype(f32)
    from1 = lax.ppermute(
        mine[PLANE : 2 * PLANE].astype(bf16), "y", [(i + 1, i) for i in range(ys - 1)]
    )
    from2 = lax.ppermute(mine[:PLANE].astype(bf16), "y", [(i + 2, i) for i in range(ys - 2)])
    summed = mine[2 * PLANE :] + from1.astype(f32) + from2.astype(f32)
    parts = lax.all_to_all(
        summed.astype(bf16).reshape(RING, ROWS, 2 * HD), ("zb", "za"), 0, 0
    )
    grad_terms = jnp.sum(parts.astype(f32), 0).astype(bf16)

    terms_y = lax.all_gather(grad_terms, "y", axis=0, tiled=True)
    dims = (RING, depth, 2 * HD)
    near, far = kernel_call(
        weight_terms,
        (shape(dims, f32), shape(dims, bf16)),
        (core, rows_y, terms_y),
        (),
        2 * ys * ROWS * quarter * 2 * HD,
    )
    summed = (near + swap(far).astype(f32)).astype(bf16)
    parts = lax.all_to_all(summed, ("zb", "za"), 0, 0)
    grads = jnp.sum(parts.astype(f32), 0)

    terms_x = lax.all_gather(grad_terms, "x", axis=0)
    input_grad = kernel_call(
        input_terms,
        shape((ROWS, quarter), f32),
        (terms_x, w_all),
        (),
        2 * ROWS * quarter * xs * 2 * HD,
    )
    return (grads[:, :HD], grads[:, HD:], input_grad)


def solution(mesh):
    fine = Mesh(
        mesh.devices.reshape(4, RING // 2, 2, 2, 4), ("y", "zb", "za", "c", "x")
    )
    ctx = ("y", "zb", "za", "c")
    split = P(ctx, "x")
    return jax.shard_map(
        body,
        mesh=fine,
        in_specs=(P(ctx, None), split, split, split, split, split, P(ctx)),
        out_specs=(split, split, split),
        check_vma=False,
    )
```

time: 636 us -> 292 us (0.46)
  waiting for transfers between devices: 442 us -> 42.4 us
  matrix products: 72.9 us -> 0 us
  blocking collectives: 38.1 us -> 109 us
  Pallas kernels: 0 us -> 53.8 us
  starting transfers between devices: 0.43 us -> 41.9 us
  local copies, waits for them, and re-layouts: 35.7 us -> 16.2 us
  other arithmetic: 28.3 us -> 13.1 us
    reduce_scatter x2 -> x0, waiting for transfers between devices: 170 us -> none  [the longest x1 146 us: body(): lax.psum_scatter(spread[(need - 1) * rows:], 'ctx', scatter_dimension=0,...]
    unnamed x6 -> x1, waiting for transfers between devices: 159 us -> 0.02 us
    all_gather x2 -> x1, waiting for transfers between devices: 113 us -> 0.01 us  [body(): w_all = lax.all_gather(turned, ('y', 'zb', 'za', 'c'), axis=0, tiled=True)]
    dot_general x12 -> x0, matrix products: 72.9 us -> none  [the longest x3 26.7 us: attend(): jnp.einsum('jtk,tjd->kd', ds, q_block, preferred_element_type=jnp.float32)]
    pallas_call x0 -> x5, Pallas kernels: none -> 53.8 us  [the longest x1 44.1 us: attention(): pl.pallas_call(attend, out_shape=(out, out), in_specs=[pl.BlockSpec(memor...]
    all_gather x1 -> x5, blocking collectives: 38.1 us -> 88 us  [the longest x1 24.5 us: body(): lax.all_gather(jnp.concatenate((w_key, counts), 0), plane_axes, axis=0)]
    ppermute x0 -> x11, starting transfers between devices: none -> 28.5 us  [the longest x6 12.9 us: swap(): return lax.ppermute(a, axis, [(0, 1), (1, 0)])]
    ppermute x0 -> x11, waiting for transfers between devices: none -> 22.8 us  [the longest x1 13.9 us: body(): lax.ppermute(mine[:PLANE].astype(bf16), 'y', [(i + 2, i) for i in range(y...]
  transfers between devices with their start and end apart: 5 -> 15, of which waited for: 5 -> 9; matrix products, arithmetic and copies ran while one was open for 5% -> 8% of each run, Pallas kernels for 0% -> 16%
where the time goes in v1:
time: 292 us; the launch traced here: 291 us
  blocking collectives  109 us (37%)
  Pallas kernels  53.8 us (18%)
  waiting for transfers between devices  42.4 us (15%)
  starting transfers between devices  41.9 us (14%)
  local copies, waits for them, and re-layouts  16.2 us (6%)
  between operations  14.2 us (5%)
  other arithmetic  13.1 us (4%)
    pallas_call x1, Pallas kernels, attention(): pl.pallas_call(attend, out_shape=(out, out), in_specs=[pl.BlockSpec(memor...  44.1 us
    all_gather x1, blocking collectives, body(): lax.all_gather(jnp.concatenate((w_key, counts), 0), plane_axes, axis=0)  24.5 us
    all_to_all x1, blocking collectives, body(): lax.all_to_all(summed.astype(bf16).reshape(RING, ROWS, 2 * HD), ('zb', 'z...  21 us
    all_gather x1, blocking collectives, body(): terms_y = lax.all_gather(grad_terms, 'y', axis=0, tiled=True)  20 us
    all_gather x1, blocking collectives, body(): value_part = lax.all_gather(tied, plane_axes, axis=0)  18 us
    all_gather x1, blocking collectives, body(): own2 = lax.all_gather(pair, 'zb', axis=0, tiled=True)  15.5 us
    ppermute x1, waiting for transfers between devices, body(): lax.ppermute(mine[:PLANE].astype(bf16), 'y', [(i + 2, i) for i in range(y...  13.9 us
    all_to_all x1, waiting for transfers between devices, body(): parts = lax.all_to_all(summed, ('zb', 'za'), 0, 0)  13.6 us
  transfers between devices with their start and end apart: 15, of which 9 were waited for; matrix products, arithmetic and copies ran while one was open for 8% of the time, Pallas kernels for 16%

profile of v1, /device:TPU:1, one launch (start us, length us, event | category | flops | bytes accessed | tf_op | source)
XLA Modules:
  0.0 290.6 jit_solution(2681181752333199415)
XLA Ops:
  7.2 4.2 %split_columns.1 = bf16[4,128,3072]{2,1,0:T(8,128)(2,1)} custom-call(bf16[128,12288]{1,0:T(8,128)(2,1)} %src.1), custom_call_target="tpu_custom_call" | custom-call | tf_op jit(solution)/shard_map/split_columns/pallas_call | solution.py:214
  11.4 5.2 %all-to-all-start = ((bf16[4,128,3072]{2,1,0:T(8,128)(2,1)}), bf16[4,128,3072]{2,1,0:T(8,128)(2,1)S(1)}, u32[]{:S(2)}, u32[]{:S(2)}) async-start(bf16[4,128,3072]{2,1,0:T(8,128)(2,1)} %split_columns.1), calls=%async_computation | async-start | bytes 6291456 | tf_op jit(solution)/shard_map/all_to_all | solution.py:242
  16.6 0.6 fusion.4
  17.2 1.4 fusion.6
  18.6 24.5 %all-gather = bf16[3328,128]{1,0:T(8,128)(2,1)} all-gather(bf16[208,128]{1,0:T(8,128)(2,1)S(1)} %fusion.3), channel_id=2, replica_groups=mesh['y'=4,'zb'=4,'za'=2,'c'=2,'x'=4] {'zb','za','c'}, dimensions={0}, use_global_device_ids=true | all-gather | bytes 905216 | tf_op jit(solution)/shard_map/all_gather | solution.py:253
  43.1 18.0 %all-gather.1 = bf16[3072,128]{1,0:T(8,128)(2,1)} all-gather(bf16[192,128]{1,0:T(8,128)(2,1)S(1)} %copy-done.6), channel_id=3, replica_groups=mesh['y'=4,'zb'=4,'za'=2,'c'=2,'x'=4] {'zb','za','c'}, dimensions={0}, use_global_device_ids=true | all-gather | bytes 835584 | tf_op jit(solution)/shard_map/all_gather | solution.py:255
  61.1 1.2 copy-done.1
  62.3 1.1 copy-done.2
  63.4 1.1 project.1
  64.5 0.0 copy-start.3
  64.5 0.8 copy-done.3
  65.3 4.6 %all-to-all-start.1 = ((f32[4,136,256]{2,1,0:T(8,128)}), f32[4,136,256]{2,1,0:T(8,128)}, u32[]{:S(2)}, u32[]{:S(2)}) async-start(f32[4,136,256]{2,1,0:T(8,128)} %copy-done.3), calls=%async_computation.1 | async-start | bytes 1114112 | tf_op jit(solution)/shard_map/all_to_all | solution.py:278
  69.9 1.5 pad_maximum_fusion.1
  71.4 2.1 collective-permute-start.10
  73.6 6.0 %all-to-all-done.1 = f32[4,136,256]{2,1,0:T(8,128)} async-done(((f32[4,136,256]{2,1,0:T(8,128)}), f32[4,136,256]{2,1,0:T(8,128)}, u32[]{:S(2)}, u32[]{:S(2)}) %all-to-all-start.1) | async-done | bytes 557088 | tf_op jit(solution)/shard_map/all_to_all | solution.py:278
  79.5 1.7 slice_reduce_fusion
  81.3 0.0 all-gather.5.cloned.1.call-update
  81.3 1.5 collective-permute-start
  82.8 1.9 collective-permute-done
  84.7 0.8 pad_maximum_fusion
  85.6 15.5 %all_gather.31.own2 = bf16[1024,256]{1,0:T(8,128)(2,1)} all-gather(bf16[256,256]{1,0:T(8,128)(2,1)S(1)} %pad_maximum_fusion), channel_id=1, replica_groups=mesh['y'=4,'zb'=4,'za'=2,'c'=2,'x'=4] {'zb'}, dimensions={0}, use_global_device_ids=true | all-gather | bytes 655360 | tf_op jit(solution)/shard_map/all_gather | solution.py:291
  101.1 3.6 %collective-permute-start.1 = (bf16[1024,256]{1,0:T(8,128)(2,1)}, bf16[1024,256]{1,0:T(8,128)(2,1)}, u32[]{:S(2)}, u32[]{:S(2)}) collective-permute-start(bf16[1024,256]{1,0:T(8,128)(2,1)} %all_gather.31.own2), channel_id=1, source_target_pairs={{0,128},{64,192},{1,129},{65,193},{2,130},{66,194},{3,131},{67,195... | collective-permute-start | bytes 1572872 | tf_op jit(solution)/shard_map/ppermute | solution.py:293
  104.6 7.4 %collective-permute-start.2 = (bf16[1024,256]{1,0:T(8,128)(2,1)}, bf16[1024,256]{1,0:T(8,128)(2,1)}, u32[]{:S(2)}, u32[]{:S(2)}) collective-permute-start(bf16[1024,256]{1,0:T(8,128)(2,1)} %all_gather.31.own2), channel_id=1, source_target_pairs={{0,64},{64,128},{128,192},{1,65},{65,129},{129,193},{2,66},{66,130... | collective-permute-start | bytes 1572872 | tf_op jit(solution)/shard_map/ppermute | solution.py:292
  112.0 0.9 copy.12
  112.9 1.2 copy.13
  114.2 2.0 copy.14
  116.1 1.9 copy.15
  118.1 1.9 copy.17
  120.0 2.1 convert_multiply_fusion
  122.0 1.2 reduce_sum.70
  123.3 4.3 %collective-permute-start.5 = (bf16[1024,256]{1,0:T(8,128)(2,1)}, bf16[1024,256]{1,0:T(8,128)(2,1)S(1)}, u32[]{:S(2)}, u32[]{:S(2)}) collective-permute-start(bf16[1024,256]{1,0:T(8,128)(2,1)} %all_gather.31.own2), channel_id=1, source_target_pairs={{0,4},{4,0},{1,5},{5,1},{2,6},{6,2},{3,7},{7,3},{8,12},{12,8},{9,1... | collective-permute-start | bytes 1572872 | tf_op jit(solution)/shard_map/ppermute | solution.py:225
  127.6 0.1 collective-permute-start.3
  127.7 0.4 collective-permute-start.4
  128.1 0.8 slice_reduce_fusion.1
  128.9 0.1 add_subtract_fusion
  129.0 0.1 pad_add_fusion.place
  129.0 0.3 collective-permute-done.5.far2
  129.3 0.7 collective-permute-done.3.far0
  130.1 0.7 collective-permute-done.4.far1
  130.8 0.7 tile.2
  131.5 1.0 copy-done.4
  132.5 44.1 %attend.1 = (bf16[3072,256]{1,0:T(8,128)(2,1)S(1)}, bf16[3072,256]{1,0:T(8,128)(2,1)}) custom-call(s32[6]{0:T(128)S(1)} %pad_add_fusion.place, bf16[1024,256]{1,0:T(8,128)(2,1)} %collective-permute-done.1.own0, bf16[1024,256]{1,0:T(8,128)(2,1)} %collective-permute-done.2.own1, bf16[1024,256]{1,0:T(8,128)(2,1)} %all_gather.31.own2, ...), custom_call_target="tpu_custom_call" | custom-call | flops 6845104128 | bytes 8388608 | tf_op jit(solution)/shard_map/attend/pallas_call | solution.py:134
  176.6 0.4 collective-permute-start.6
  177.0 3.2 %collective-permute-done.6 = bf16[3072,256]{1,0:T(8,128)(2,1)S(1)} collective-permute-done((bf16[3072,256]{1,0:T(8,128)(2,1)}, bf16[3072,256]{1,0:T(8,128)(2,1)S(1)}, u32[]{:S(2)}, u32[]{:S(2)}) %collective-permute-start.6) | collective-permute-done | bytes 1572896 | tf_op jit(solution)/shard_map/ppermute | solution.py:225
  180.2 0.4 fusion.7
  180.6 0.1 fusion.8
  180.7 1.3 collective-permute-start.8
  182.0 1.3 collective-permute-start.7
  183.3 13.9 %collective-permute-done.8 = bf16[1024,256]{1,0:T(8,128)(2,1)S(1)} collective-permute-done((bf16[1024,256]{1,0:T(8,128)(2,1)S(1)}, bf16[1024,256]{1,0:T(8,128)(2,1)S(1)}, u32[]{:S(2)}, u32[]{:S(2)}) %collective-permute-start.8) | collective-permute-done | bytes 524320 | tf_op jit(solution)/shard_map/ppermute | solution.py:304
  197.2 0.2 fusion.1
  197.4 21.0 %all_to_all.20 = bf16[8,128,256]{2,1,0:T(8,128)(2,1)} all-to-all(bf16[8,128,256]{2,1,0:T(8,128)(2,1)S(1)} %bitcast.30), channel_id=1, replica_groups=mesh['y'=4,'zb'=4,'za'=2,'c'=2,'x'=4] {'zb','za'}, dimensions={0} | all-to-all | bytes 1048576 | tf_op jit(solution)/shard_map/all_to_all | solution.py:306
  218.5 1.1 reduce_sum.71
  219.6 20.0 %all_gather.32.terms_ref = bf16[512,256]{1,0:T(8,128)(2,1)S(1)} all-gather(bf16[128,256]{1,0:T(8,128)(2,1)S(1)} %reduce_sum.71), channel_id=1, replica_groups=mesh['y'=4,'zb'=4,'za'=2,'c'=2,'x'=4] {'y'}, dimensions={0}, use_global_device_ids=true | all-gather | bytes 327680 | tf_op jit(solution)/shard_map/all_gather | solution.py:311
  239.6 1.0 weight_terms.1
  240.6 6.2 %collective-permute-start.9 = (bf16[8,192,256]{2,1,0:T(8,128)(2,1)S(1)}, bf16[8,192,256]{2,1,0:T(8,128)(2,1)S(1)}, u32[]{:S(2)}, u32[]{:S(2)}) collective-permute-start(bf16[8,192,256]{2,1,0:T(8,128)(2,1)S(1)} %get-tuple-element.27), channel_id=1, source_target_pairs={{0,4},{4,0},{1,5},{5,1},{2,6},{6,2},{3,7},{7,3},{8,12},{12,8},{9,1... | collective-permute-start | bytes 2359304 | tf_op jit(solution)/shard_map/ppermute | solution.py:225
  246.8 1.9 collective-permute-done.9
  248.7 1.1 add_convert_fusion
  249.8 3.5 %all-to-all-start.3 = ((bf16[8,192,256]{2,1,0:T(8,128)(2,1)}), bf16[8,192,256]{2,1,0:T(8,128)(2,1)S(1)}, u32[]{:S(2)}, u32[]{:S(2)}) async-start(bf16[8,192,256]{2,1,0:T(8,128)(2,1)} %add_convert_fusion), calls=%async_computation.3 | async-start | bytes 1572864 | tf_op jit(solution)/shard_map/all_to_all | solution.py:321
  253.3 10.0 %all-gather.2 = bf16[512,256]{1,0:T(8,128)(2,1)S(1)} all-gather(bf16[128,256]{1,0:T(8,128)(2,1)S(1)} %reduce_sum.71), channel_id=4, replica_groups=mesh['y'=4,'zb'=4,'za'=2,'c'=2,'x'=4] {'x'}, dimensions={0}, use_global_device_ids=true | all-gather | bytes 327680 | tf_op jit(solution)/shard_map/all_gather | solution.py:324
  263.3 13.6 %all-to-all-done.3 = bf16[8,192,256]{2,1,0:T(8,128)(2,1)S(1)} async-done(((bf16[8,192,256]{2,1,0:T(8,128)(2,1)}), bf16[8,192,256]{2,1,0:T(8,128)(2,1)S(1)}, u32[]{:S(2)}, u32[]{:S(2)}) %all-to-all-start.3) | async-done | bytes 786464 | tf_op jit(solution)/shard_map/all_to_all | solution.py:321
  276.9 0.1 convert_reduce_fusion
  277.0 0.7 fusion.9
  277.7 2.8 copy-done
  280.5 3.3 %input_terms.1 = f32[128,3072]{1,0:T(8,128)} custom-call(bf16[4,128,256]{2,1,0:T(8,128)(2,1)S(1)} %bitcast.24, bf16[4,3072,256]{2,1,0:T(8,128)(2,1)S(1)} %bitcast.21), custom_call_target="tpu_custom_call" | custom-call | flops 805306368 | bytes 8388608 | tf_op jit(solution)/shard_map/input_terms/pallas_call | solution.py:196
  (22 shorter events, 0.1 us)
Async XLA Ops:
  11.4 5.2 %copy-start.8 = (s32[128]{0:T(128)S(1)}, s32[128]{0:T(128)}, u32[]{:S(2)}) copy-start(s32[128]{0:T(128)} %param.15) | copy-start | bytes 1540
  11.4 7.2 %copy-start.7 = (bf16[192,128]{1,0:T(8,128)(2,1)S(1)}, bf16[192,128]{1,0:T(8,128)(2,1)}, u32[]{:S(2)}) copy-start(bf16[192,128]{1,0:T(8,128)(2,1)} %param.10) | copy-start | bytes 147460
  11.4 31.7 %copy-start.6 = (bf16[192,128]{1,0:T(8,128)(2,1)S(1)}, bf16[192,128]{1,0:T(8,128)(2,1)}, u32[]{:S(2)}) copy-start(bf16[192,128]{1,0:T(8,128)(2,1)} %param.11) | copy-start | bytes 147460
  11.4 49.7 %all-to-all-start = ((bf16[4,128,3072]{2,1,0:T(8,128)(2,1)}), bf16[4,128,3072]{2,1,0:T(8,128)(2,1)S(1)}, u32[]{:S(2)}, u32[]{:S(2)}) async-start(bf16[4,128,3072]{2,1,0:T(8,128)(2,1)} %split_columns.1), calls=%async_computation | async-start | bytes 6291456 | tf_op jit(solution)/shard_map/all_to_all | solution.py:242
  61.1 1.2 copy-start.1
  62.3 1.1 copy-start.2
  64.5 0.8 copy-start.3
  65.3 46.7 %copy-start.5 = (bf16[128,1536]{1,0:T(8,128)(2,1)S(1)}, bf16[128,1536]{1,0:T(8,128)(2,1)}, u32[]{:S(2)}) copy-start(bf16[128,1536]{1,0:T(8,128)(2,1)} %param.12) | copy-start | bytes 1179652
  65.3 14.3 %all-to-all-start.1 = ((f32[4,136,256]{2,1,0:T(8,128)}), f32[4,136,256]{2,1,0:T(8,128)}, u32[]{:S(2)}, u32[]{:S(2)}) async-start(f32[4,136,256]{2,1,0:T(8,128)} %copy-done.3), calls=%async_computation.1 | async-start | bytes 1114112 | tf_op jit(solution)/shard_map/all_to_all | solution.py:278
  69.9 207.7 %all-gather.5.cloned.1.call-start = ((), (), s32[]{:S(2)}) async-start(), calls=%async_computation.4 | async-start | bytes 6389760 | tf_op jit(solution)/shard_map/all_gather | solution.py:287
  71.4 9.9 %collective-permute-start.10 = (bf16[192,256]{1,0:T(8,128)(2,1)}, bf16[192,256]{1,0:T(8,128)(2,1)}, u32[]{:S(2)}, u32[]{:S(2)}) collective-permute-start(bf16[192,256]{1,0:T(8,128)(2,1)} %pad_maximum_fusion.1), channel_id=1, source_target_pairs={{0,0},{1,64},{2,128},{3,192},{64,1},{65,65},{66,129},{67,193},{128... | collective-permute-start | bytes 294920 | tf_op jit(solution)/shard_map/ppermute | solution.py:244
  81.3 3.4 %collective-permute-start = (bf16[128,256]{1,0:T(8,128)(2,1)}, bf16[128,256]{1,0:T(8,128)(2,1)S(1)}, u32[]{:S(2)}, u32[]{:S(2)}) collective-permute-start(bf16[128,256]{1,0:T(8,128)(2,1)} %slice_reduce_fusion), channel_id=1, source_target_pairs={{0,8},{8,0},{1,9},{9,1},{2,10},{10,2},{3,11},{11,3},{4,12},{12,4},... | collective-permute-start | bytes 196616 | tf_op jit(solution)/shard_map/ppermute | solution.py:225
  101.1 26.5 %collective-permute-start.1 = (bf16[1024,256]{1,0:T(8,128)(2,1)}, bf16[1024,256]{1,0:T(8,128)(2,1)}, u32[]{:S(2)}, u32[]{:S(2)}) collective-permute-start(bf16[1024,256]{1,0:T(8,128)(2,1)} %all_gather.31.own2), channel_id=1, source_target_pairs={{0,128},{64,192},{1,129},{65,193},{2,130},{66,194},{3,131},{67,195... | collective-permute-start | bytes 1572872 | tf_op jit(solution)/shard_map/ppermute | solution.py:293
  104.6 23.1 %collective-permute-start.2 = (bf16[1024,256]{1,0:T(8,128)(2,1)}, bf16[1024,256]{1,0:T(8,128)(2,1)}, u32[]{:S(2)}, u32[]{:S(2)}) collective-permute-start(bf16[1024,256]{1,0:T(8,128)(2,1)} %all_gather.31.own2), channel_id=1, source_target_pairs={{0,64},{64,128},{128,192},{1,65},{65,129},{129,193},{2,66},{66,130... | collective-permute-start | bytes 1572872 | tf_op jit(solution)/shard_map/ppermute | solution.py:292
  123.3 6.1 %collective-permute-start.5 = (bf16[1024,256]{1,0:T(8,128)(2,1)}, bf16[1024,256]{1,0:T(8,128)(2,1)S(1)}, u32[]{:S(2)}, u32[]{:S(2)}) collective-permute-start(bf16[1024,256]{1,0:T(8,128)(2,1)} %all_gather.31.own2), channel_id=1, source_target_pairs={{0,4},{4,0},{1,5},{5,1},{2,6},{6,2},{3,7},{7,3},{8,12},{12,8},{9,1... | collective-permute-start | bytes 1572872 | tf_op jit(solution)/shard_map/ppermute | solution.py:225
  127.6 2.5 collective-permute-start.3
  127.7 3.1 %collective-permute-start.4 = (bf16[1024,256]{1,0:T(8,128)(2,1)}, bf16[1024,256]{1,0:T(8,128)(2,1)S(1)}, u32[]{:S(2)}, u32[]{:S(2)}) collective-permute-start(bf16[1024,256]{1,0:T(8,128)(2,1)} %collective-permute-done.2.own1), channel_id=1, source_target_pairs={{0,4},{4,0},{1,5},{5,1},{2,6},{6,2},{3,7},{7,3},{8,12},{12,8},{9,1... | collective-permute-start | bytes 1572872 | tf_op jit(solution)/shard_map/ppermute | solution.py:225
  131.5 1.0 copy-start.4
  176.6 3.6 %collective-permute-start.6 = (bf16[3072,256]{1,0:T(8,128)(2,1)}, bf16[3072,256]{1,0:T(8,128)(2,1)S(1)}, u32[]{:S(2)}, u32[]{:S(2)}) collective-permute-start(bf16[3072,256]{1,0:T(8,128)(2,1)} %get-tuple-element.25), channel_id=1, source_target_pairs={{0,4},{4,0},{1,5},{5,1},{2,6},{6,2},{3,7},{7,3},{8,12},{12,8},{9,1... | collective-permute-start | bytes 4718600 | tf_op jit(solution)/shard_map/ppermute | solution.py:225
  180.7 16.5 %collective-permute-start.8 = (bf16[1024,256]{1,0:T(8,128)(2,1)S(1)}, bf16[1024,256]{1,0:T(8,128)(2,1)S(1)}, u32[]{:S(2)}, u32[]{:S(2)}) collective-permute-start(bf16[1024,256]{1,0:T(8,128)(2,1)S(1)} %get-tuple-element.34), channel_id=1, source_target_pairs={{128,0},{192,64},{129,1},{193,65},{130,2},{194,66},{131,3},{195,67... | collective-permute-start | bytes 1572872 | tf_op jit(solution)/shard_map/ppermute | solution.py:304
  182.0 15.2 %collective-permute-start.7 = (bf16[1024,256]{1,0:T(8,128)(2,1)S(1)}, bf16[1024,256]{1,0:T(8,128)(2,1)S(1)}, u32[]{:S(2)}, u32[]{:S(2)}) collective-permute-start(bf16[1024,256]{1,0:T(8,128)(2,1)S(1)} %get-tuple-element.33), channel_id=1, source_target_pairs={{64,0},{128,64},{192,128},{65,1},{129,65},{193,129},{66,2},{130,66... | collective-permute-start | bytes 1572872 | tf_op jit(solution)/shard_map/ppermute | solution.py:301
  240.6 8.1 %collective-permute-start.9 = (bf16[8,192,256]{2,1,0:T(8,128)(2,1)S(1)}, bf16[8,192,256]{2,1,0:T(8,128)(2,1)S(1)}, u32[]{:S(2)}, u32[]{:S(2)}) collective-permute-start(bf16[8,192,256]{2,1,0:T(8,128)(2,1)S(1)} %get-tuple-element.27), channel_id=1, source_target_pairs={{0,4},{4,0},{1,5},{5,1},{2,6},{6,2},{3,7},{7,3},{8,12},{12,8},{9,1... | collective-permute-start | bytes 2359304 | tf_op jit(solution)/shard_map/ppermute | solution.py:225
  249.8 27.1 %all-to-all-start.3 = ((bf16[8,192,256]{2,1,0:T(8,128)(2,1)}), bf16[8,192,256]{2,1,0:T(8,128)(2,1)S(1)}, u32[]{:S(2)}, u32[]{:S(2)}) async-start(bf16[8,192,256]{2,1,0:T(8,128)(2,1)} %add_convert_fusion), calls=%async_computation.3 | async-start | bytes 1572864 | tf_op jit(solution)/shard_map/all_to_all | solution.py:321
  277.7 2.8 copy-start
Sparse Core Ops, SparseCore 0:
  81.4 85.4 all-gather.4

commit v2 on v1

--- a/solution.py
+++ b/solution.py
@@ -60,75 +60,56 @@
     start = jnp.where(doc == 0, place[3], jnp.where(doc == 1, place[4], place[5]))
     low = jnp.maximum(start, token + 1)
     row = lax.broadcasted_iota(jnp.int32, (PAIR, TILE), 0)
-
-    for g in range(q_ref.shape[0] // TILE):
-        q = q_ref[g * TILE : (g + 1) * TILE, :]
-        o = o_ref[g * TILE : (g + 1) * TILE, :]
+    dk_s[...] = jnp.zeros_like(dk_s)
+    dv_s[...] = jnp.zeros_like(dv_s)
+
+    @pl.loop(0, q_ref.shape[0] // TILE)
+    def heads(g):
+        tile = pl.ds(pl.multiple_of(g * TILE, TILE), TILE)
+        q = q_ref[tile, :]
+        o = o_ref[tile, :]
         delta = delta_ref[g]
-
-        def first(j, carry, q=q):
-            top, total = carry
-            at = pl.ds(pl.multiple_of(j * PAIR, PAIR), PAIR)
+        top = jnp.full((1, TILE), HIDDEN, jnp.float32)
+        total = jnp.zeros((1, TILE), jnp.float32)
+        for j in range(CHUNKS):
+            at = slice(j * PAIR, (j + 1) * PAIR)
             s = dot(k_s[at, :], q, NT)
-            seen = (row >= low - j * PAIR) & (row <= high - j * PAIR)
+            seen = row >= low - j * PAIR
+            if (j + 1) * PAIR > WINDOW:
+                seen = seen & (row <= high - j * PAIR)
             s = jnp.where(seen, s, HIDDEN)
             peak = jnp.maximum(top, jnp.max(s, 0, keepdims=True))
             p = jnp.exp2((s - peak) * RATE)
             p_s[at, :] = p
             m_s[j] = peak
             total = total * jnp.exp2((top - peak) * RATE) + jnp.sum(p, 0, keepdims=True)
-            return peak, total
-
-        top, total = lax.fori_loop(
-            0,
-            CHUNKS,
-            first,
-            (jnp.full((1, TILE), HIDDEN, jnp.float32), jnp.zeros((1, TILE), jnp.float32)),
-        )
+            top = peak
         share = 1.0 / total
-
-        def second(j, carry, g=g, q=q, o=o, delta=delta, top=top, share=share):
-            at = pl.ds(pl.multiple_of(j * PAIR, PAIR), PAIR)
+        for j in range(CHUNKS):
+            at = slice(j * PAIR, (j + 1) * PAIR)
             p = p_s[at, :] * (jnp.exp2((m_s[j] - top) * RATE) * share)
             dp = dot(v_s[at, :], o, NT)
             ds = (p * (dp - delta)).astype(jnp.bfloat16)
-            dv = dot(p.astype(jnp.bfloat16), o, NN)
-            dk = dot(ds, q, NN)
-            if g == 0:
-                dv_s[at, :] = dv
-                dk_s[at, :] = dk
-            else:
-                dv_s[at, :] += dv
-                dk_s[at, :] += dk
-            return carry
-
-        lax.fori_loop(0, CHUNKS, second, 0)
-
-    for plane in range(3):
-
-        @pl.loop(0, RING)
-        def store(step, plane=plane):
-            j = plane * RING + step + odd * (1 - 2 * (step % 2)) - z
-            block = plane * RING + step + odd * (1 - 2 * (step % 2))
-            dst = pl.ds(pl.multiple_of(block * ROWS, ROWS), ROWS)
-            inside = (j >= 0) & (j < CHUNKS)
-
-            @pl.when(inside)
-            def _():
-                for slot, ref in enumerate((near_out, far_out)):
-                    core = c if slot == 0 else 1 - c
-                    src = pl.ds(pl.multiple_of(j * PAIR + core * ROWS, ROWS), ROWS)
-                    ref[dst, :HD] = (dk_s[src, :] * SCALE).astype(jnp.bfloat16)
-                    ref[dst, HD:] = dv_s[src, :].astype(jnp.bfloat16)
-
-            @pl.when(jnp.logical_not(inside))
-            def _():
-                for ref in (near_out, far_out):
-                    ref[dst, :] = jnp.zeros((ROWS, 2 * HD), jnp.bfloat16)
+            dv_s[at, :] += dot(p.astype(jnp.bfloat16), o, NN)
+            dk_s[at, :] += dot(ds, q, NN)
+
+    def give(j, block):
+        for slot, ref in enumerate((near_out, far_out)):
+            core = c if slot == 0 else 1 - c
+            src = pl.ds(pl.multiple_of(j * PAIR + core * ROWS, ROWS), ROWS)
+            ref[block, :, :HD] = (dk_s[src, :] * SCALE).astype(jnp.bfloat16)
+            ref[block, :, HD:] = dv_s[src, :].astype(jnp.bfloat16)
+
+    @pl.loop(0, RING)
+    def store(step):
+        give(jnp.where(step > z, step - z, step - z + 2 * RING), 2 * step)
+        give(RING + step - z, 2 * step + 1)
+
+    give(0, 2 * RING)
 
 
 def attention(place, kv, q, o, delta, doc):
-    out = jax.ShapeDtypeStruct((3 * PLANE, 2 * HD), jnp.bfloat16)
+    out = jax.ShapeDtypeStruct((2 * RING + 1, ROWS, 2 * HD), jnp.bfloat16)
     heads = q.shape[0] // ROWS
     vmem = pl.BlockSpec(memory_space=pltpu.VMEM)
     return pl.pallas_call(
@@ -154,14 +135,16 @@
     )(place, *kv, q, o, delta, doc)
 
 
-def project(rows_ref, key_ref, value_ref, sent, w_s):
-    depth = value_ref.shape[1]
-    blocks = value_ref.shape[0]
+def project(core, rows_ref, own_ref, far_ref, sent, w_s):
+    depth = w_s.shape[0] // (2 * RING)
     counts = jnp.zeros((8, HD), jnp.float32)
-    for i in range(blocks):
-        w_s[i * depth : (i + 1) * depth, :HD] = key_ref[i, :depth, :]
-        w_s[i * depth : (i + 1) * depth, HD:] = value_ref[i]
-        counts = counts + key_ref[i, depth:, :].astype(jnp.float32)[:8]
+    for slot, ref in enumerate((own_ref, far_ref)):
+        c = core[0] if slot == 0 else 1 - core[0]
+        for i in range(RING):
+            at = pl.ds(pl.multiple_of((2 * i + c) * depth, depth), depth)
+            w_s[at, :HD] = ref[i, :depth, :]
+            w_s[at, HD:] = ref[i, depth : 2 * depth, :]
+            counts = counts + ref[i, 2 * depth :, :].astype(jnp.float32)[:8]
     rows = rows_ref[...].reshape(-1, rows_ref.shape[2])
     places = rows_ref.shape[0]
     sent[:, :ROWS, :] = dot(rows, w_s[...], NN).reshape(places, ROWS, 2 * HD)
@@ -249,10 +232,10 @@
 
     before = jnp.stack([jnp.sum(doc_ids < 1), jnp.sum(doc_ids < 2)]).astype(f32)
     counts = jnp.zeros((16, HD), f32).at[0, :2].set(before).astype(bf16)
-    plane_axes = ("zb", "za", "c")
-    key_part = lax.all_gather(jnp.concatenate((w_key, counts), 0), plane_axes, axis=0)
-    key_part, tied = lax.optimization_barrier((key_part, w_value))
-    value_part = lax.all_gather(tied, plane_axes, axis=0)
+    w_own = lax.all_gather(
+        jnp.concatenate((w_key, w_value, counts), 0), ("zb", "za"), axis=0
+    )
+    w_far = swap(w_own)
 
     def by_head(a):
         return a.reshape(ROWS, heads, HD).swapaxes(0, 1)
@@ -271,7 +254,7 @@
     sent = kernel_call(
         project,
         shape((ys, ROWS + 8, 2 * HD), f32),
-        (rows_y, key_part, value_part),
+        (core, rows_y, w_own, w_far),
         [pltpu.VMEM((quarter, 2 * HD), bf16)],
         2 * ys * ROWS * quarter * 2 * HD,
     )
@@ -297,18 +280,19 @@
         window, (own0, own1, own2, far0, far1, far2), q_rows, o_rows, delta, doc_tile
     )
 
-    mine = near.astype(f32) + swap(far).astype(f32)
-    from1 = lax.ppermute(
-        mine[PLANE : 2 * PLANE].astype(bf16), "y", [(i + 1, i) for i in range(ys - 1)]
-    )
-    from2 = lax.ppermute(mine[:PLANE].astype(bf16), "y", [(i + 2, i) for i in range(ys - 2)])
-    summed = mine[2 * PLANE :] + from1.astype(f32) + from2.astype(f32)
-    parts = lax.all_to_all(
-        summed.astype(bf16).reshape(RING, ROWS, 2 * HD), ("zb", "za"), 0, 0
-    )
-    grad_terms = jnp.sum(parts.astype(f32), 0).astype(bf16)
-
-    terms_y = lax.all_gather(grad_terms, "y", axis=0, tiled=True)
+    mine = (near.astype(f32) + swap(far).astype(f32)).astype(bf16)
+    ring = ("zb", "za")
+    parts = lax.all_to_all(mine[:-1].reshape(RING, 2, ROWS, 2 * HD), ring, 0, 0)
+    parts = parts.astype(f32)
+    here = (jnp.arange(RING) >= z).astype(f32)[:, None, None]
+    back = (jnp.sum((1 - here) * parts[:, 0], 0) + mine[-1].astype(f32)).astype(bf16)
+    back = jnp.stack((jnp.sum(here * parts[:, 0], 0), jnp.sum(parts[:, 1], 0))).astype(bf16), back[None]
+    sums = lax.all_gather(jnp.concatenate(back), "y", axis=0).astype(f32)
+    sums = jnp.pad(sums, ((0, 2), (0, 0), (0, 0), (0, 0)))
+    terms_y = (sums[:ys, 0] + sums[1 : ys + 1, 1] + sums[2 : ys + 2, 2]).astype(bf16)
+    grad_terms = lax.dynamic_index_in_dim(terms_y, y, 0, keepdims=False)
+
+    terms_y = terms_y.reshape(ys * ROWS, 2 * HD)
     dims = (RING, depth, 2 * HD)
     near, far = kernel_call(
         weight_terms,
@@ -318,8 +302,7 @@
         2 * ys * ROWS * quarter * 2 * HD,
     )
     summed = (near + swap(far).astype(f32)).astype(bf16)
-    parts = lax.all_to_all(summed, ("zb", "za"), 0, 0)
-    grads = jnp.sum(parts.astype(f32), 0)
+    parts = lax.all_to_all(summed, ring, 0, 0)
 
     terms_x = lax.all_gather(grad_terms, "x", axis=0)
     input_grad = kernel_call(
@@ -329,6 +312,8 @@
         (),
         2 * ROWS * quarter * xs * 2 * HD,
     )
+    parts, input_grad = lax.optimization_barrier((parts, input_grad))
+    grads = jnp.sum(parts.astype(f32), 0)
     return (grads[:, :HD], grads[:, HD:], input_grad)
 
 

time: 292 us -> 250 us (0.86)
  blocking collectives: 109 us -> 65.8 us
  Pallas kernels: 53.8 us -> 35.5 us
  waiting for transfers between devices: 42.4 us -> 52.3 us
  starting transfers between devices: 41.9 us -> 50.1 us
    all_gather x3 -> x2, blocking collectives: 62.5 us -> 39.3 us  [the longest x1 27.3 us: body(): lax.all_gather(jnp.concatenate((w_key, w_value, counts), 0), ('zb', 'za')...]
    all_to_all x1 -> x2, waiting for transfers between devices: 13.6 us -> 36.7 us  [the longest x1 29.2 us: body(): parts = lax.all_to_all(mine[:-1].reshape(RING, 2, ROWS, 2 * HD), ring, 0, 0)]
    all_to_all x1 -> x0, blocking collectives: 21 us -> none  [body(): lax.all_to_all(summed.astype(bf16).reshape(RING, ROWS, 2 * HD), ('zb', 'z...]
    pallas_call x1, Pallas kernels: 44.1 us -> 24.4 us  [attention(): pl.pallas_call(attend, out_shape=(out, out), in_specs=[pl.BlockSpec(memor...]
    ppermute x2 -> x0, waiting for transfers between devices: 13.9 us -> none  [the longest x1 13.9 us: body(): lax.ppermute(mine[:PLANE].astype(bf16), 'y', [(i + 2, i) for i in range(y...]
    ppermute x6 -> x7, starting transfers between devices: 12.9 us -> 19.2 us  [swap(): return lax.ppermute(a, axis, [(0, 1), (1, 0)])]
    ppermute x1, starting transfers between devices: 3.55 us -> 8.09 us  [body(): own0 = lax.ppermute(own2, 'y', [(i, i + 2) for i in range(ys - 2)])]
    ppermute x1, starting transfers between devices: 7.41 us -> 3.07 us  [body(): own1 = lax.ppermute(own2, 'y', [(i, i + 1) for i in range(ys - 1)])]
  transfers between devices with their start and end apart: 15 -> 15, of which waited for: 9 -> 8; matrix products, arithmetic and copies ran while one was open for 8% -> 10% of each run, Pallas kernels for 16% -> 12%
where the time goes in v2:
time: 250 us; the launch traced here: 249 us
  blocking collectives  65.8 us (26%)
  waiting for transfers between devices  52.3 us (21%)
  starting transfers between devices  50.1 us (20%)
  Pallas kernels  35.5 us (14%)
  local copies, waits for them, and re-layouts  16 us (6%)
  other arithmetic  14.6 us (6%)
  between operations  14.2 us (6%)
    all_to_all x1, waiting for transfers between devices, body(): parts = lax.all_to_all(mine[:-1].reshape(RING, 2, ROWS, 2 * HD), ring, 0, 0)  29.2 us
    all_gather x1, blocking collectives, body(): lax.all_gather(jnp.concatenate((w_key, w_value, counts), 0), ('zb', 'za')...  27.3 us
    pallas_call x1, Pallas kernels, attention(): pl.pallas_call(attend, out_shape=(out, out), in_specs=[pl.BlockSpec(memor...  24.4 us
    ppermute x7, starting transfers between devices, swap(): return lax.ppermute(a, axis, [(0, 1), (1, 0)])  19.2 us
    all_gather x1, blocking collectives, body(): own2 = lax.all_gather(pair, 'zb', axis=0, tiled=True)  16.5 us
    all_gather x1, blocking collectives, body(): sums = lax.all_gather(jnp.concatenate(back), 'y', axis=0).astype(f32)  12.1 us
    ppermute x7, waiting for transfers between devices, swap(): return lax.ppermute(a, axis, [(0, 1), (1, 0)])  10.5 us
    unnamed x19, local copies, waits for them, and re-layouts  10.4 us
  transfers between devices with their start and end apart: 15, of which 8 were waited for; matrix products, arithmetic and copies ran while one was open for 10% of the time, Pallas kernels for 12%

profile of v2, /device:TPU:1, one launch (start us, length us, event | category | flops | bytes accessed | tf_op | source)
XLA Modules:
  0.0 248.6 jit_solution(10019104459113331684)
XLA Ops:
  7.2 4.2 %split_columns.1 = bf16[4,128,3072]{2,1,0:T(8,128)(2,1)} custom-call(bf16[128,12288]{1,0:T(8,128)(2,1)} %src.1), custom_call_target="tpu_custom_call" | custom-call | tf_op jit(solution)/shard_map/split_columns/pallas_call | solution.py:197
  11.4 5.2 %all-to-all-start = ((bf16[4,128,3072]{2,1,0:T(8,128)(2,1)}), bf16[4,128,3072]{2,1,0:T(8,128)(2,1)S(1)}, u32[]{:S(2)}, u32[]{:S(2)}) async-start(bf16[4,128,3072]{2,1,0:T(8,128)(2,1)} %split_columns.1), calls=%async_computation | async-start | bytes 6291456 | tf_op jit(solution)/shard_map/all_to_all | solution.py:225
  16.5 0.6 fusion.6
  17.2 1.4 fusion.8
  18.5 27.3 %all-gather = bf16[3200,128]{1,0:T(8,128)(2,1)} all-gather(bf16[400,128]{1,0:T(8,128)(2,1)S(1)} %fusion.5), channel_id=2, replica_groups=mesh['y'=4,'zb'=4,'za'=2,'c'=2,'x'=4] {'zb','za'}, dimensions={0}, use_global_device_ids=true | all-gather | bytes 921600 | tf_op jit(solution)/shard_map/all_gather | solution.py:235
  45.8 5.5 %collective-permute-start = (bf16[8,400,128]{2,1,0:T(8,128)(2,1)}, bf16[8,400,128]{2,1,0:T(8,128)(2,1)}, u32[]{:S(2)}, u32[]{:S(2)}) collective-permute-start(bf16[8,400,128]{2,1,0:T(8,128)(2,1)} %bitcast.5.own_ref), channel_id=1, source_target_pairs={{0,4},{4,0},{1,5},{5,1},{2,6},{6,2},{3,7},{7,3},{8,12},{12,8},{9,1... | collective-permute-start | bytes 2457608 | tf_op jit(solution)/shard_map/ppermute | solution.py:208
  51.3 2.3 collective-permute-done.far_ref
  53.6 2.6 %project.1 = f32[4,136,256]{2,1,0:T(8,128)S(1)} custom-call(s32[1]{0:T(128)} %bitcast.core, bf16[4,128,3072]{2,1,0:T(8,128)(2,1)S(1)} %all-to-all-done.rows_ref, bf16[8,400,128]{2,1,0:T(8,128)(2,1)} %bitcast.5.own_ref, bf16[8,400,128]{2,1,0:T(8,128)(2,1)} %collective-permute-done.far_ref), custom_call_target="tpu_custom_call" | custom-call | flops 805306368 | bytes 8388608 | tf_op jit(solution)/shard_map/project/pallas_call | solution.py:179
  56.3 0.8 copy-done.1
  57.1 4.7 %all-to-all-start.1 = ((f32[4,136,256]{2,1,0:T(8,128)}), f32[4,136,256]{2,1,0:T(8,128)}, u32[]{:S(2)}, u32[]{:S(2)}) async-start(f32[4,136,256]{2,1,0:T(8,128)} %copy-done.1), calls=%async_computation.1 | async-start | bytes 1114112 | tf_op jit(solution)/shard_map/all_to_all | solution.py:261
  61.7 1.5 pad_maximum_fusion.2
  63.2 2.1 collective-permute-start.9
  65.3 5.0 %all-to-all-done.1 = f32[4,136,256]{2,1,0:T(8,128)} async-done(((f32[4,136,256]{2,1,0:T(8,128)}), f32[4,136,256]{2,1,0:T(8,128)}, u32[]{:S(2)}, u32[]{:S(2)}) %all-to-all-start.1) | async-done | bytes 557088 | tf_op jit(solution)/shard_map/all_to_all | solution.py:261
  70.4 1.7 slice_reduce_fusion.1
  72.1 0.0 all-gather.5.cloned.1.call-update
  72.1 0.4 collective-permute-start.1
  72.5 3.1 %collective-permute-done.1 = bf16[128,256]{1,0:T(8,128)(2,1)S(1)} collective-permute-done((bf16[128,256]{1,0:T(8,128)(2,1)}, bf16[128,256]{1,0:T(8,128)(2,1)S(1)}, u32[]{:S(2)}, u32[]{:S(2)}) %collective-permute-start.1) | collective-permute-done | bytes 65568 | tf_op jit(solution)/shard_map/ppermute | solution.py:208
  75.6 0.8 pad_maximum_fusion.1
  76.4 16.5 %all_gather.24.own2 = bf16[1024,256]{1,0:T(8,128)(2,1)} all-gather(bf16[256,256]{1,0:T(8,128)(2,1)S(1)} %pad_maximum_fusion.1), channel_id=1, replica_groups=mesh['y'=4,'zb'=4,'za'=2,'c'=2,'x'=4] {'zb'}, dimensions={0}, use_global_device_ids=true | all-gather | bytes 655360 | tf_op jit(solution)/shard_map/all_gather | solution.py:274
  92.9 8.1 %collective-permute-start.2 = (bf16[1024,256]{1,0:T(8,128)(2,1)}, bf16[1024,256]{1,0:T(8,128)(2,1)}, u32[]{:S(2)}, u32[]{:S(2)}) collective-permute-start(bf16[1024,256]{1,0:T(8,128)(2,1)} %all_gather.24.own2), channel_id=1, source_target_pairs={{0,128},{64,192},{1,129},{65,193},{2,130},{66,194},{3,131},{67,195... | collective-permute-start | bytes 1572872 | tf_op jit(solution)/shard_map/ppermute | solution.py:276
  101.0 3.1 %collective-permute-start.3 = (bf16[1024,256]{1,0:T(8,128)(2,1)}, bf16[1024,256]{1,0:T(8,128)(2,1)}, u32[]{:S(2)}, u32[]{:S(2)}) collective-permute-start(bf16[1024,256]{1,0:T(8,128)(2,1)} %all_gather.24.own2), channel_id=1, source_target_pairs={{0,64},{64,128},{128,192},{1,65},{65,129},{129,193},{2,66},{66,130... | collective-permute-start | bytes 1572872 | tf_op jit(solution)/shard_map/ppermute | solution.py:275
  104.1 0.9 copy.20
  105.0 1.2 copy.21
  106.2 2.0 copy.22
  108.2 2.0 copy.23
  110.1 1.9 copy.25
  112.1 2.1 convert_multiply_fusion
  114.2 1.2 reduce_sum.87
  115.4 6.3 %collective-permute-start.6 = (bf16[1024,256]{1,0:T(8,128)(2,1)}, bf16[1024,256]{1,0:T(8,128)(2,1)S(1)}, u32[]{:S(2)}, u32[]{:S(2)}) collective-permute-start(bf16[1024,256]{1,0:T(8,128)(2,1)} %all_gather.24.own2), channel_id=1, source_target_pairs={{0,4},{4,0},{1,5},{5,1},{2,6},{6,2},{3,7},{7,3},{8,12},{12,8},{9,1... | collective-permute-start | bytes 1572872 | tf_op jit(solution)/shard_map/ppermute | solution.py:208
  121.7 0.1 collective-permute-start.4
  121.8 2.5 %collective-permute-start.5 = (bf16[1024,256]{1,0:T(8,128)(2,1)}, bf16[1024,256]{1,0:T(8,128)(2,1)S(1)}, u32[]{:S(2)}, u32[]{:S(2)}) collective-permute-start(bf16[1024,256]{1,0:T(8,128)(2,1)} %collective-permute-done.3.own1), channel_id=1, source_target_pairs={{0,4},{4,0},{1,5},{5,1},{2,6},{6,2},{3,7},{7,3},{8,12},{12,8},{9,1... | collective-permute-start | bytes 1572872 | tf_op jit(solution)/shard_map/ppermute | solution.py:208
  124.4 0.8 slice_reduce_fusion.2
  125.1 0.1 add_subtract_fusion
  125.2 0.1 pad_add_fusion.place
  125.3 0.8 collective-permute-done.5.far1
  126.1 0.7 tile.2
  126.8 1.0 copy-done.2
  127.8 24.4 %attend.1 = (bf16[17,128,256]{2,1,0:T(8,128)(2,1)S(1)}, bf16[17,128,256]{2,1,0:T(8,128)(2,1)S(1)}) custom-call(s32[6]{0:T(128)S(1)} %pad_add_fusion.place, bf16[1024,256]{1,0:T(8,128)(2,1)} %collective-permute-done.2.own0, bf16[1024,256]{1,0:T(8,128)(2,1)} %collective-permute-done.3.own1, bf16[1024,256]{1,0:T(8,128)(2,1)} %all_gather.24.own2, ...), custom_call_target="tpu_custom_call" | custom-call | flops 6845104128 | bytes 8388608 | tf_op jit(solution)/shard_map/attend/pallas_call | solution.py:115
  152.1 0.4 collective-permute-start.7
  152.5 2.5 collective-permute-done.7
  155.0 0.4 add_convert_fusion
  155.3 0.0 copy-start.3
  155.4 1.0 copy-done.3
  156.3 1.1 slice.68
  157.4 4.2 %all-to-all-start.2 = ((bf16[8,2,128,256]{3,2,1,0:T(8,128)(2,1)}), bf16[8,2,128,256]{3,2,1,0:T(8,128)(2,1)}, u32[]{:S(2)}, u32[]{:S(2)}) async-start(bf16[8,2,128,256]{3,2,1,0:T(8,128)(2,1)} %bitcast.45), calls=%async_computation.2 | async-start | bytes 2097152 | tf_op jit(solution)/shard_map/all_to_all | solution.py:285
  161.7 29.2 %all-to-all-done.2 = bf16[8,2,128,256]{3,2,1,0:T(8,128)(2,1)} async-done(((bf16[8,2,128,256]{3,2,1,0:T(8,128)(2,1)}), bf16[8,2,128,256]{3,2,1,0:T(8,128)(2,1)}, u32[]{:S(2)}, u32[]{:S(2)}) %all-to-all-start.2) | async-done | bytes 1048608 | tf_op jit(solution)/shard_map/all_to_all | solution.py:285
  190.9 1.4 convert_element_type.91
  192.3 0.1 slice_reduce_fusion
  192.4 0.2 multiply_reduce_fusion.1
  192.6 0.9 fusion.4
  193.5 12.1 %all-gather.1 = bf16[12,128,256]{2,1,0:T(8,128)(2,1)S(1)} all-gather(bf16[3,128,256]{2,1,0:T(8,128)(2,1)S(1)} %pad_maximum_fusion), channel_id=3, replica_groups=mesh['y'=4,'zb'=4,'za'=2,'c'=2,'x'=4] {'y'}, dimensions={0}, use_global_device_ids=true | all-gather | bytes 983040 | tf_op jit(solution)/shard_map/all_gather | solution.py:290
  205.6 0.1 convert.15
  205.7 0.1 fusion.2
  205.8 1.0 weight_terms.1
  206.8 4.0 %collective-permute-start.8 = (bf16[8,192,256]{2,1,0:T(8,128)(2,1)S(1)}, bf16[8,192,256]{2,1,0:T(8,128)(2,1)S(1)}, u32[]{:S(2)}, u32[]{:S(2)}) collective-permute-start(bf16[8,192,256]{2,1,0:T(8,128)(2,1)S(1)} %get-tuple-element.25), channel_id=1, source_target_pairs={{0,4},{4,0},{1,5},{5,1},{2,6},{6,2},{3,7},{7,3},{8,12},{12,8},{9,1... | collective-permute-start | bytes 2359304 | tf_op jit(solution)/shard_map/ppermute | solution.py:208
  210.9 1.9 collective-permute-done.8
  212.8 1.1 add_convert_fusion.1
  213.8 3.5 %all-to-all-start.3 = ((bf16[8,192,256]{2,1,0:T(8,128)(2,1)}), bf16[8,192,256]{2,1,0:T(8,128)(2,1)S(1)}, u32[]{:S(2)}, u32[]{:S(2)}) async-start(bf16[8,192,256]{2,1,0:T(8,128)(2,1)} %add_convert_fusion.1), calls=%async_computation.3 | async-start | bytes 1572864 | tf_op jit(solution)/shard_map/all_to_all | solution.py:305
  217.4 10.0 %all-gather.2 = bf16[4,1,128,256]{3,2,1,0:T(8,128)(2,1)S(1)} all-gather(bf16[1,1,128,256]{3,2,1,0:T(8,128)(2,1)S(1)} %constant_dynamic-slice_fusion), channel_id=4, replica_groups=mesh['y'=4,'zb'=4,'za'=2,'c'=2,'x'=4] {'x'}, dimensions={0}, use_global_device_ids=true | all-gather | bytes 327680 | tf_op jit(solution)/shard_map/all_gather | solution.py:307
  227.4 2.8 %copy-done = bf16[12288,256]{1,0:T(8,128)(2,1)S(1)} copy-done((bf16[12288,256]{1,0:T(8,128)(2,1)S(1)}, bf16[12288,256]{1,0:T(8,128)(2,1)}, u32[]{:S(2)}) %copy-start) | copy-done | bytes 6291480
  230.2 3.3 %input_terms.1 = f32[128,3072]{1,0:T(8,128)} custom-call(bf16[4,128,256]{2,1,0:T(8,128)(2,1)S(1)} %bitcast.41, bf16[4,3072,256]{2,1,0:T(8,128)(2,1)S(1)} %bitcast.39), custom_call_target="tpu_custom_call" | custom-call | flops 805306368 | bytes 8388608 | tf_op jit(solution)/shard_map/input_terms/pallas_call | solution.py:179
  233.4 7.5 %all-to-all-done.3 = bf16[8,192,256]{2,1,0:T(8,128)(2,1)S(1)} async-done(((bf16[8,192,256]{2,1,0:T(8,128)(2,1)}), bf16[8,192,256]{2,1,0:T(8,128)(2,1)S(1)}, u32[]{:S(2)}, u32[]{:S(2)}) %all-to-all-start.3) | async-done | bytes 786464 | tf_op jit(solution)/shard_map/all_to_all | solution.py:305
  240.9 0.1 convert_reduce_fusion
  241.0 0.7 fusion.9
  (26 shorter events, 0.1 us)
Async XLA Ops:
  11.4 5.2 %copy-start.7 = (s32[128]{0:T(128)S(1)}, s32[128]{0:T(128)}, u32[]{:S(2)}) copy-start(s32[128]{0:T(128)} %param.15) | copy-start | bytes 1540
  11.4 7.2 %copy-start.5 = (bf16[192,128]{1,0:T(8,128)(2,1)S(1)}, bf16[192,128]{1,0:T(8,128)(2,1)}, u32[]{:S(2)}) copy-start(bf16[192,128]{1,0:T(8,128)(2,1)} %param.11) | copy-start | bytes 147460
  11.4 7.2 %copy-start.6 = (bf16[192,128]{1,0:T(8,128)(2,1)S(1)}, bf16[192,128]{1,0:T(8,128)(2,1)}, u32[]{:S(2)}) copy-start(bf16[192,128]{1,0:T(8,128)(2,1)} %param.10) | copy-start | bytes 147460
  11.4 42.3 %all-to-all-start = ((bf16[4,128,3072]{2,1,0:T(8,128)(2,1)}), bf16[4,128,3072]{2,1,0:T(8,128)(2,1)S(1)}, u32[]{:S(2)}, u32[]{:S(2)}) async-start(bf16[4,128,3072]{2,1,0:T(8,128)(2,1)} %split_columns.1), calls=%async_computation | async-start | bytes 6291456 | tf_op jit(solution)/shard_map/all_to_all | solution.py:225
  45.8 7.8 %collective-permute-start = (bf16[8,400,128]{2,1,0:T(8,128)(2,1)}, bf16[8,400,128]{2,1,0:T(8,128)(2,1)}, u32[]{:S(2)}, u32[]{:S(2)}) collective-permute-start(bf16[8,400,128]{2,1,0:T(8,128)(2,1)} %bitcast.5.own_ref), channel_id=1, source_target_pairs={{0,4},{4,0},{1,5},{5,1},{2,6},{6,2},{3,7},{7,3},{8,12},{12,8},{9,1... | collective-permute-start | bytes 2457608 | tf_op jit(solution)/shard_map/ppermute | solution.py:208
  56.3 0.8 copy-start.1
  57.1 47.0 %copy-start.4 = (bf16[128,1536]{1,0:T(8,128)(2,1)S(1)}, bf16[128,1536]{1,0:T(8,128)(2,1)}, u32[]{:S(2)}) copy-start(bf16[128,1536]{1,0:T(8,128)(2,1)} %param.12) | copy-start | bytes 1179652
  57.1 13.3 %all-to-all-start.1 = ((f32[4,136,256]{2,1,0:T(8,128)}), f32[4,136,256]{2,1,0:T(8,128)}, u32[]{:S(2)}, u32[]{:S(2)}) async-start(f32[4,136,256]{2,1,0:T(8,128)} %copy-done.1), calls=%async_computation.1 | async-start | bytes 1114112 | tf_op jit(solution)/shard_map/all_to_all | solution.py:261
  61.7 165.6 %all-gather.5.cloned.1.call-start = ((), (), s32[]{:S(2)}) async-start(), calls=%async_computation.4 | async-start | bytes 6389760 | tf_op jit(solution)/shard_map/all_gather | solution.py:270
  63.2 8.9 %collective-permute-start.9 = (bf16[192,256]{1,0:T(8,128)(2,1)}, bf16[192,256]{1,0:T(8,128)(2,1)}, u32[]{:S(2)}, u32[]{:S(2)}) collective-permute-start(bf16[192,256]{1,0:T(8,128)(2,1)} %pad_maximum_fusion.2), channel_id=1, source_target_pairs={{0,0},{1,64},{2,128},{3,192},{64,1},{65,65},{66,129},{67,193},{128... | collective-permute-start | bytes 294920 | tf_op jit(solution)/shard_map/ppermute | solution.py:227
  72.1 3.4 %collective-permute-start.1 = (bf16[128,256]{1,0:T(8,128)(2,1)}, bf16[128,256]{1,0:T(8,128)(2,1)S(1)}, u32[]{:S(2)}, u32[]{:S(2)}) collective-permute-start(bf16[128,256]{1,0:T(8,128)(2,1)} %slice_reduce_fusion.1), channel_id=1, source_target_pairs={{0,8},{8,0},{1,9},{9,1},{2,10},{10,2},{3,11},{11,3},{4,12},{12,4},... | collective-permute-start | bytes 196616 | tf_op jit(solution)/shard_map/ppermute | solution.py:208
  92.9 28.8 %collective-permute-start.2 = (bf16[1024,256]{1,0:T(8,128)(2,1)}, bf16[1024,256]{1,0:T(8,128)(2,1)}, u32[]{:S(2)}, u32[]{:S(2)}) collective-permute-start(bf16[1024,256]{1,0:T(8,128)(2,1)} %all_gather.24.own2), channel_id=1, source_target_pairs={{0,128},{64,192},{1,129},{65,193},{2,130},{66,194},{3,131},{67,195... | collective-permute-start | bytes 1572872 | tf_op jit(solution)/shard_map/ppermute | solution.py:276
  101.0 20.8 %collective-permute-start.3 = (bf16[1024,256]{1,0:T(8,128)(2,1)}, bf16[1024,256]{1,0:T(8,128)(2,1)}, u32[]{:S(2)}, u32[]{:S(2)}) collective-permute-start(bf16[1024,256]{1,0:T(8,128)(2,1)} %all_gather.24.own2), channel_id=1, source_target_pairs={{0,64},{64,128},{128,192},{1,65},{65,129},{129,193},{2,66},{66,130... | collective-permute-start | bytes 1572872 | tf_op jit(solution)/shard_map/ppermute | solution.py:275
  115.4 9.9 %collective-permute-start.6 = (bf16[1024,256]{1,0:T(8,128)(2,1)}, bf16[1024,256]{1,0:T(8,128)(2,1)S(1)}, u32[]{:S(2)}, u32[]{:S(2)}) collective-permute-start(bf16[1024,256]{1,0:T(8,128)(2,1)} %all_gather.24.own2), channel_id=1, source_target_pairs={{0,4},{4,0},{1,5},{5,1},{2,6},{6,2},{3,7},{7,3},{8,12},{12,8},{9,1... | collective-permute-start | bytes 1572872 | tf_op jit(solution)/shard_map/ppermute | solution.py:208
  121.7 3.6 %collective-permute-start.4 = (bf16[1024,256]{1,0:T(8,128)(2,1)}, bf16[1024,256]{1,0:T(8,128)(2,1)S(1)}, u32[]{:S(2)}, u32[]{:S(2)}) collective-permute-start(bf16[1024,256]{1,0:T(8,128)(2,1)} %collective-permute-done.2.own0), channel_id=1, source_target_pairs={{0,4},{4,0},{1,5},{5,1},{2,6},{6,2},{3,7},{7,3},{8,12},{12,8},{9,1... | collective-permute-start | bytes 1572872 | tf_op jit(solution)/shard_map/ppermute | solution.py:208
  121.8 4.3 %collective-permute-start.5 = (bf16[1024,256]{1,0:T(8,128)(2,1)}, bf16[1024,256]{1,0:T(8,128)(2,1)S(1)}, u32[]{:S(2)}, u32[]{:S(2)}) collective-permute-start(bf16[1024,256]{1,0:T(8,128)(2,1)} %collective-permute-done.3.own1), channel_id=1, source_target_pairs={{0,4},{4,0},{1,5},{5,1},{2,6},{6,2},{3,7},{7,3},{8,12},{12,8},{9,1... | collective-permute-start | bytes 1572872 | tf_op jit(solution)/shard_map/ppermute | solution.py:208
  126.8 1.0 copy-start.2
  152.1 2.8 %collective-permute-start.7 = (bf16[17,128,256]{2,1,0:T(8,128)(2,1)S(1)}, bf16[17,128,256]{2,1,0:T(8,128)(2,1)S(1)}, u32[]{:S(2)}, u32[]{:S(2)}) collective-permute-start(bf16[17,128,256]{2,1,0:T(8,128)(2,1)S(1)} %get-tuple-element.23), channel_id=1, source_target_pairs={{0,4},{4,0},{1,5},{5,1},{2,6},{6,2},{3,7},{7,3},{8,12},{12,8},{9,1... | collective-permute-start | bytes 3342344 | tf_op jit(solution)/shard_map/ppermute | solution.py:208
  155.3 1.0 copy-start.3
  157.4 33.5 %all-to-all-start.2 = ((bf16[8,2,128,256]{3,2,1,0:T(8,128)(2,1)}), bf16[8,2,128,256]{3,2,1,0:T(8,128)(2,1)}, u32[]{:S(2)}, u32[]{:S(2)}) async-start(bf16[8,2,128,256]{3,2,1,0:T(8,128)(2,1)} %bitcast.45), calls=%async_computation.2 | async-start | bytes 2097152 | tf_op jit(solution)/shard_map/all_to_all | solution.py:285
  206.8 5.9 %collective-permute-start.8 = (bf16[8,192,256]{2,1,0:T(8,128)(2,1)S(1)}, bf16[8,192,256]{2,1,0:T(8,128)(2,1)S(1)}, u32[]{:S(2)}, u32[]{:S(2)}) collective-permute-start(bf16[8,192,256]{2,1,0:T(8,128)(2,1)S(1)} %get-tuple-element.25), channel_id=1, source_target_pairs={{0,4},{4,0},{1,5},{5,1},{2,6},{6,2},{3,7},{7,3},{8,12},{12,8},{9,1... | collective-permute-start | bytes 2359304 | tf_op jit(solution)/shard_map/ppermute | solution.py:208
  213.8 27.1 %all-to-all-start.3 = ((bf16[8,192,256]{2,1,0:T(8,128)(2,1)}), bf16[8,192,256]{2,1,0:T(8,128)(2,1)S(1)}, u32[]{:S(2)}, u32[]{:S(2)}) async-start(bf16[8,192,256]{2,1,0:T(8,128)(2,1)} %add_convert_fusion.1), calls=%async_computation.3 | async-start | bytes 1572864 | tf_op jit(solution)/shard_map/all_to_all | solution.py:305
  227.4 2.8 %copy-start = (bf16[12288,256]{1,0:T(8,128)(2,1)S(1)}, bf16[12288,256]{1,0:T(8,128)(2,1)}, u32[]{:S(2)}) copy-start(bf16[12288,256]{1,0:T(8,128)(2,1)} %all-gather.5.cloned.1.call-done) | copy-start | bytes 18874372
Sparse Core Ops, SparseCore 0:
  72.3 87.9 all-gather.4

commit v3 on v2

v3 whole, which is shorter than its diff:
```python
import math

import jax
import jax.numpy as jnp
from jax import lax
from jax.experimental import pallas as pl
from jax.experimental.pallas import tpu as pltpu
from jax.sharding import Mesh
from jax.sharding import PartitionSpec as P

HD = 128
WINDOW = 4096
ROWS = 128
PAIR = 2 * ROWS
RING = 8
CHUNKS = WINDOW // PAIR + 1
SPAN = CHUNKS * PAIR
GROUP = 4
TILE = GROUP * ROWS
SCALE = 1.0 / math.sqrt(HD)
RATE = SCALE * math.log2(math.e)
HIDDEN = -1e30

NT = (((1,), (1,)), ((), ()))
NN = (((1,), (0,)), ((), ()))
TN = (((0,), (0,)), ((), ()))


def dot(a, b, dims):
    return lax.dot_general(a, b, dims, preferred_element_type=jnp.float32)


def attend(
    place, own, far, own_back, far_back, q_ref, o_ref, a_ref, doc_ref,
    near_out, far_out, near_back, far_out_back, k_s, v_s, p_s, m_s, dk_s, dv_s,
):
    z = place[0]
    c = place[1]

    def rows(j, slot):
        core = c if slot == 0 else 1 - c
        return pl.ds(pl.multiple_of(j * PAIR + core * ROWS, ROWS), ROWS)

    def merged(step):
        return jnp.where(step > z, step - z, step - z + 2 * RING)

    def take(j, slot, block):
        k_s[rows(j, slot), :] = block[:, :HD]
        v_s[rows(j, slot), :] = block[:, HD:]

    @pl.loop(0, RING)
    def load(step):
        for slot, ref in enumerate((own, far)):
            take(merged(step), slot, ref[step, 0])
            take(RING + step - z, slot, ref[step, 1])

    take(0, 0, own_back[...])
    take(0, 1, far_back[...])

    doc = doc_ref[...]
    token = c * ROWS + lax.broadcasted_iota(jnp.int32, (1, TILE), 1) % ROWS
    high = token + WINDOW
    start = jnp.where(doc == 0, place[2], jnp.where(doc == 1, place[3], place[4]))
    low = jnp.maximum(start, token + 1)
    row = lax.broadcasted_iota(jnp.int32, (PAIR, TILE), 0)
    dk_s[...] = jnp.zeros_like(dk_s)
    dv_s[...] = jnp.zeros_like(dv_s)

    @pl.loop(0, q_ref.shape[1] // TILE)
    def heads(g):
        def by_head(ref):
            at = [pl.ds(pl.multiple_of(g * TILE + h * HD, HD), HD) for h in range(GROUP)]
            return [ref[:, one] for one in at]

        q = jnp.concatenate(by_head(q_ref), 0)
        o_heads = by_head(o_ref)
        o = jnp.concatenate(o_heads, 0)
        products = [
            one.astype(jnp.float32) * two.astype(jnp.float32)
            for one, two in zip(o_heads, by_head(a_ref))
        ]
        delta = jnp.concatenate([jnp.sum(p.T, 0, keepdims=True) for p in products], 1)
        top = jnp.full((1, TILE), HIDDEN, jnp.float32)
        total = jnp.zeros((1, TILE), jnp.float32)
        for j in range(CHUNKS):
            at = slice(j * PAIR, (j + 1) * PAIR)
            s = dot(k_s[at, :], q, NT)
            seen = row >= low - j * PAIR
            if (j + 1) * PAIR > WINDOW:
                seen = seen & (row <= high - j * PAIR)
            s = jnp.where(seen, s, HIDDEN)
            peak = jnp.maximum(top, jnp.max(s, 0, keepdims=True))
            p = jnp.exp2((s - peak) * RATE)
            p_s[at, :] = p
            m_s[j] = peak
            total = total * jnp.exp2((top - peak) * RATE) + jnp.sum(p, 0, keepdims=True)
            top = peak
        share = 1.0 / total
        for j in range(CHUNKS):
            at = slice(j * PAIR, (j + 1) * PAIR)
            p = p_s[at, :] * (jnp.exp2((m_s[j] - top) * RATE) * share)
            dp = dot(v_s[at, :], o, NT)
            ds = (p * (dp - delta)).astype(jnp.bfloat16)
            dv_s[at, :] += dot(p.astype(jnp.bfloat16), o, NN)
            dk_s[at, :] += dot(ds, q, NN)

    def give(j, slot):
        src = rows(j, slot)
        dk = (dk_s[src, :] * SCALE).astype(jnp.bfloat16)
        return jnp.concatenate((dk, dv_s[src, :].astype(jnp.bfloat16)), 1)

    @pl.loop(0, RING)
    def store(step):
        for slot, ref in enumerate((near_out, far_out)):
            ref[step, 0] = give(merged(step), slot)
            ref[step, 1] = give(RING + step - z, slot)

    near_back[...] = give(0, 0)
    far_out_back[...] = give(0, 1)


def attention(place, kv, q, o, a, doc):
    out = jax.ShapeDtypeStruct((RING, 2, ROWS, 2 * HD), jnp.bfloat16)
    back = jax.ShapeDtypeStruct((ROWS, 2 * HD), jnp.bfloat16)
    heads = q.shape[1] // HD
    vmem = pl.BlockSpec(memory_space=pltpu.VMEM)
    return pl.pallas_call(
        attend,
        out_shape=(out, out, back, back),
        in_specs=[pl.BlockSpec(memory_space=pltpu.SMEM)] + [vmem] * 8,
        out_specs=(vmem,) * 4,
        scratch_shapes=[
            pltpu.VMEM((SPAN, HD), jnp.bfloat16),
            pltpu.VMEM((SPAN, HD), jnp.bfloat16),
            pltpu.VMEM((SPAN, TILE), jnp.float32),
            pltpu.VMEM((CHUNKS, 1, TILE), jnp.float32),
            pltpu.VMEM((SPAN, HD), jnp.float32),
            pltpu.VMEM((SPAN, HD), jnp.float32),
        ],
        compiler_params=pltpu.CompilerParams(vmem_limit_bytes=48 << 20),
        cost_estimate=pl.CostEstimate(
            flops=8 * heads * ROWS * SPAN * HD,
            bytes_accessed=8 << 20,
            transcendentals=heads * ROWS * SPAN,
        ),
        name="attend",
    )(place, *kv, q, o, a, doc)


def project(core, rows_ref, own_ref, far_ref, sent, w_s):
    depth = w_s.shape[0] // (2 * RING)
    counts = jnp.zeros((8, HD), jnp.float32)
    for slot, ref in enumerate((own_ref, far_ref)):
        c = core[0] if slot == 0 else 1 - core[0]
        for i in range(RING):
            at = pl.ds(pl.multiple_of((2 * i + c) * depth, depth), depth)
            w_s[at, :HD] = ref[i, :depth, :]
            w_s[at, HD:] = ref[i, depth : 2 * depth, :]
            counts = counts + ref[i, 2 * depth :, :].astype(jnp.float32)[:8]
    rows = rows_ref[...].reshape(-1, rows_ref.shape[2])
    places = rows_ref.shape[0]
    sent[:, :ROWS, :] = dot(rows, w_s[...], NN).reshape(places, ROWS, 2 * HD)
    sent[:, ROWS:, :HD] = jnp.broadcast_to(counts[None], (places, 8, HD))
    sent[:, ROWS:, HD:] = jnp.zeros((places, 8, HD), jnp.float32)


def window_sums(place, parts_ref, back_ref, out):
    same = jnp.zeros((ROWS, 2 * HD), jnp.float32)
    after = same
    last = back_ref[...]
    for step in range(RING):
        block = parts_ref[step, 0].astype(jnp.float32)
        mine = step >= place[0]
        same = same + jnp.where(mine, block, 0.0)
        last = last + jnp.where(mine, 0.0, block)
        after = after + parts_ref[step, 1].astype(jnp.float32)
    for i, total in enumerate((same, after, last)):
        out[i] = total.astype(jnp.bfloat16)


def weight_terms(place, rows_ref, sums_ref, near, far, own_terms):
    c = place[0]
    depth = near.shape[1]
    places = sums_ref.shape[0]
    blocks = []
    for i in range(places):
        total = sums_ref[i, 0].astype(jnp.float32)
        for k in range(1, min(3, places - i)):
            total = total + sums_ref[i + k, k].astype(jnp.float32)
        blocks.append(total.astype(jnp.bfloat16))

        @pl.when(place[1] == i)
        def _(block=blocks[i]):
            own_terms[...] = block

    terms = jnp.concatenate(blocks, 0)
    for z in range(RING):
        cols = rows_ref[:, :, z * 2 * depth : (z + 1) * 2 * depth]
        block = dot(cols.reshape(-1, 2 * depth), terms, TN)
        lower, upper = block[:depth], block[depth:]
        near[z] = jnp.where(c == 0, lower, upper)
        far[z] = jnp.where(c == 0, upper, lower).astype(jnp.bfloat16)


def input_terms(place, terms_ref, *refs):
    w_refs, out = refs[:-1], refs[-1]
    pieces = len(w_refs) // 2
    heads = terms_ref.shape[0]
    depth = w_refs[0].shape[1]
    even = place[0] == 0
    for z in range(RING):
        total = jnp.zeros((ROWS, 2 * depth), jnp.float32)
        for k in range(heads):
            upper = z // (RING // 2)
            at = k if k < 2 else (2 + upper if k == 2 else k + 1)
            block = z % (RING // 2) if k == 2 else z
            own, far = w_refs[at][block], w_refs[pieces + at][block]
            w = jnp.concatenate((jnp.where(even, own, far), jnp.where(even, far, own)), 0)
            total = total + dot(terms_ref[(place[1] + heads - k) % heads], w, NT)
        out[:, 2 * z * depth : 2 * (z + 1) * depth] = total


def kernel_call(f, out_shape, inputs, scratch=(), flops=0):
    smem, vmem = pl.BlockSpec(memory_space=pltpu.SMEM), pl.BlockSpec(memory_space=pltpu.VMEM)
    return pl.pallas_call(
        f,
        out_shape=out_shape,
        in_specs=[smem if a.ndim == 1 else vmem for a in inputs],
        out_specs=jax.tree.map(lambda _: vmem, out_shape),
        scratch_shapes=scratch,
        compiler_params=pltpu.CompilerParams(vmem_limit_bytes=40 << 20),
        cost_estimate=pl.CostEstimate(flops=flops, bytes_accessed=8 << 20, transcendentals=0),
        name=f.__name__,
    )(*inputs)


def split_columns(a, parts):
    rows, width = a.shape[0], a.shape[1] // parts

    def move(src, dst):
        dst[0] = src[...]

    return pl.pallas_call(
        move,
        grid=(parts,),
        out_shape=jax.ShapeDtypeStruct((parts, rows, width), a.dtype),
        in_specs=[pl.BlockSpec((rows, width), lambda i: (0, i))],
        out_specs=pl.BlockSpec((1, rows, width), lambda i: (i, 0, 0)),
        name="split_columns",
    )(a)


def swap(a, axis="c"):
    return lax.ppermute(a, axis, [(0, 1), (1, 0)])


def body(tokens_in, w_key, w_value, queries, out_grad, attn_out, doc_ids):
    f32, bf16 = jnp.float32, jnp.bfloat16
    y, zb, za, c = (lax.axis_index(name) for name in ("y", "zb", "za", "c"))
    z = zb * 2 + za
    ys = lax.axis_size("y")
    xs = lax.axis_size("x")
    depth = w_key.shape[0]
    model = tokens_in.shape[1]
    shape = jax.ShapeDtypeStruct
    core = c.astype(jnp.int32)[None]
    place = jnp.stack([z, c]).astype(jnp.int32)

    cut = split_columns(tokens_in, ys)
    rows_y = lax.all_to_all(cut, "y", 0, 0)

    turned = lax.ppermute(
        jnp.concatenate((w_key, w_value), 1),
        ("y", "x"),
        [(a * xs + b, b * xs + a) for a in range(ys) for b in range(xs)],
    )

    before = jnp.stack([jnp.sum(doc_ids < 1), jnp.sum(doc_ids < 2)]).astype(f32)
    counts = jnp.zeros((16, HD), f32).at[0, :2].set(before).astype(bf16)
    w_near = lax.all_gather(
        jnp.concatenate((w_key, w_value, counts), 0), ("zb", "za"), axis=0
    )
    w_other = swap(w_near)

    doc_tile = jnp.tile(doc_ids, GROUP)[None]

    quarter = model // ys
    sent = kernel_call(
        project,
        shape((ys, ROWS + 8, 2 * HD), f32),
        (core, rows_y, w_near, w_other),
        [pltpu.VMEM((quarter, 2 * HD), bf16)],
        2 * ys * ROWS * quarter * 2 * HD,
    )
    got = lax.all_to_all(sent, "y", 0, 0)
    kv = jnp.sum(got[:, :ROWS], 0).astype(bf16)
    starts = jnp.sum(got[:, ROWS], 0)

    origin = (y * RING + z - WINDOW // PAIR) * PAIR
    starts = jnp.concatenate((jnp.zeros((1,), jnp.int32), starts[:2].astype(jnp.int32)))
    window = jnp.concatenate((place, starts - origin))

    ring = ("zb", "za")
    before1 = lax.ppermute(kv, "y", [(i, i + 1) for i in range(ys - 1)])
    before2 = lax.ppermute(kv, "y", [(i, i + 2) for i in range(ys - 2)])
    onward = (jnp.arange(RING) >= z)[:, None, None]
    send = jnp.stack(
        (
            jnp.where(onward, kv[None], before2[None]),
            jnp.broadcast_to(before1[None], (RING, ROWS, 2 * HD)),
        ),
        1,
    )
    own = lax.all_to_all(send, ring, 0, 0)

    turned, own = lax.optimization_barrier((turned, own))
    w_z = lax.all_to_all(jnp.broadcast_to(turned[None], (RING, *turned.shape)), ring, 0, 0)

    near, far, near_back, far_back = attention(
        window, (own, swap(own), before2, swap(before2)), queries, out_grad, attn_out, doc_tile
    )

    mine = (near.astype(f32) + swap(far).astype(f32)).astype(bf16)
    mine_back = near_back.astype(f32) + swap(far_back).astype(f32)
    w_z, mine = lax.optimization_barrier((w_z, mine))
    parts = lax.all_to_all(mine, ring, 0, 0)

    def along(a, k):
        return lax.ppermute(a, "y", [(i, (i + k) % ys) for i in range(ys)])

    w_1, w_3 = along(w_z, 1), along(w_z, 3)
    half = RING // 2
    w_2 = along(w_1[:half], 1), along(w_3[half:], 3)
    parts, w_z, w_1, w_3, *w_2 = lax.optimization_barrier((parts, w_z, w_1, w_3, *w_2))
    w_own = [w_z, w_1, *w_2, w_3]
    w_far = [swap(one) for one in w_own]
    sums = kernel_call(
        window_sums,
        shape((3, ROWS, 2 * HD), bf16),
        (place, parts, mine_back),
    )
    sums = lax.all_gather(sums, "y", axis=0)

    dims = (RING, depth, 2 * HD)
    near, far, grad_terms = kernel_call(
        weight_terms,
        (shape(dims, f32), shape(dims, bf16), shape((ROWS, 2 * HD), bf16)),
        (jnp.stack([c, y]).astype(jnp.int32), rows_y, sums),
        (),
        2 * ys * ROWS * quarter * 2 * HD,
    )
    summed = (near + swap(far).astype(f32)).astype(bf16)
    parts = lax.all_to_all(summed, ring, 0, 0)

    tied, *w_far = lax.optimization_barrier((grad_terms, *w_far))
    terms_x = lax.all_gather(tied, "x", axis=0)
    input_grad = kernel_call(
        input_terms,
        shape((ROWS, quarter), f32),
        (jnp.stack([c, y]).astype(jnp.int32), terms_x, *w_own, *w_far),
        (),
        2 * ROWS * quarter * xs * 2 * HD,
    )
    parts, input_grad = lax.optimization_barrier((parts, input_grad))
    grads = jnp.sum(parts.astype(f32), 0)
    return (grads[:, :HD], grads[:, HD:], input_grad)


def solution(mesh):
    fine = Mesh(
        mesh.devices.reshape(4, RING // 2, 2, 2, 4), ("y", "zb", "za", "c", "x")
    )
    ctx = ("y", "zb", "za", "c")
    split = P(ctx, "x")
    return jax.shard_map(
        body,
        mesh=fine,
        in_specs=(P(ctx, None), split, split, split, split, split, P(ctx)),
        out_specs=(split, split, split),
        check_vma=False,
    )
```

time: 250 us -> 241 us (0.964)
  waiting for transfers between devices: 52.3 us -> 70.2 us
  blocking collectives: 65.8 us -> 49.5 us
  starting transfers between devices: 50.1 us -> 64.8 us
  between operations: 14.2 us -> 0.84 us
  local copies, waits for them, and re-layouts: 16 us -> 7.31 us
  other arithmetic: 14.6 us -> 9.01 us
  Pallas kernels: 35.5 us -> 38.6 us
    ppermute x2 -> x6, waiting for transfers between devices: 0.01 us -> 22.7 us  [the longest x4 21.3 us: along(): return lax.ppermute(a, 'y', [(i, (i + k) % ys) for i in range(ys)])]
    all_gather x3 -> x2, blocking collectives: 38.5 us -> 22.3 us  [the longest x1 11.4 us: body(): sums = lax.all_gather(sums, 'y', axis=0)]
    all_to_all x1 -> x3, starting transfers between devices: 4.24 us -> 17.6 us  [the longest x1 6.79 us: body(): parts = lax.all_to_all(mine, ring, 0, 0)]
    all_to_all x1, waiting for transfers between devices: 7.5 us -> 2.25 us  [body(): parts = lax.all_to_all(summed, ring, 0, 0)]
    unnamed x19 -> x24, local copies, waits for them, and re-layouts: 10.4 us -> 5.58 us
    all_to_all x1 -> x3, waiting for transfers between devices: 29.2 us -> 25 us  [the longest x1 25 us: body(): own = lax.all_to_all(send, ring, 0, 0)]
    all_to_all x1, waiting for transfers between devices: 5.04 us -> 8.67 us  [body(): got = lax.all_to_all(sent, 'y', 0, 0)]
    pallas_call x3 -> x4, Pallas kernels: 6.96 us -> 10.4 us  [kernel_call(): pl.pallas_call(f, out_shape=out_shape, in_specs=[smem if a.ndim == 1 else...]
  transfers between devices with their start and end apart: 15 -> 24, of which waited for: 8 -> 14; matrix products, arithmetic and copies ran while one was open for 10% -> 2% of each run, Pallas kernels for 12% -> 12%
where the time goes in v3:
time: 241 us; the launch traced here: 240 us
  waiting for transfers between devices  70.2 us (29%)
  starting transfers between devices  64.8 us (27%)
  blocking collectives  49.5 us (21%)
  Pallas kernels  38.6 us (16%)
  other arithmetic  9.01 us (4%)
  local copies, waits for them, and re-layouts  7.31 us (3%)
    all_gather x1, blocking collectives, body(): lax.all_gather(jnp.concatenate((w_key, w_value, counts), 0), ('zb', 'za')...  27.3 us
    all_to_all x1, waiting for transfers between devices, body(): own = lax.all_to_all(send, ring, 0, 0)  25 us
    pallas_call x1, Pallas kernels, attention(): pl.pallas_call(attend, out_shape=(out, out, back, back), in_specs=[pl.Blo...  24 us
    ppermute x4, waiting for transfers between devices, along(): return lax.ppermute(a, 'y', [(i, (i + k) % ys) for i in range(ys)])  21.3 us
    ppermute x11, starting transfers between devices, swap(): return lax.ppermute(a, axis, [(0, 1), (1, 0)])  19.9 us
    ppermute x11, waiting for transfers between devices, swap(): return lax.ppermute(a, axis, [(0, 1), (1, 0)])  11.6 us
    all_gather x1, blocking collectives, body(): sums = lax.all_gather(sums, 'y', axis=0)  11.4 us
    all_gather x1, blocking collectives, body(): terms_x = lax.all_gather(tied, 'x', axis=0)  10.9 us
  transfers between devices with their start and end apart: 24, of which 14 were waited for; matrix products, arithmetic and copies ran while one was open for 2% of the time, Pallas kernels for 12%

profile of v3, /device:TPU:1, one launch (start us, length us, event | category | flops | bytes accessed | tf_op | source)
XLA Modules:
  0.0 240.3 jit_solution(13391029568963594875)
XLA Ops:
  0.6 4.2 %split_columns.1 = bf16[4,128,3072]{2,1,0:T(8,128)(2,1)} custom-call(bf16[128,12288]{1,0:T(8,128)(2,1)} %src.1), custom_call_target="tpu_custom_call" | custom-call | tf_op jit(solution)/shard_map/split_columns/pallas_call | solution.py:243
  4.8 5.2 %all-to-all-start = ((bf16[4,128,3072]{2,1,0:T(8,128)(2,1)}), bf16[4,128,3072]{2,1,0:T(8,128)(2,1)S(1)}, u32[]{:S(2)}, u32[]{:S(2)}) async-start(bf16[4,128,3072]{2,1,0:T(8,128)(2,1)} %split_columns.1), calls=%async_computation | async-start | bytes 6291456 | tf_op jit(solution)/shard_map/all_to_all | solution.py:270
  10.0 0.6 fusion.2
  10.6 1.4 fusion.4
  12.0 27.3 %all-gather = bf16[3200,128]{1,0:T(8,128)(2,1)} all-gather(bf16[400,128]{1,0:T(8,128)(2,1)S(1)} %fusion.1), channel_id=2, replica_groups=mesh['y'=4,'zb'=4,'za'=2,'c'=2,'x'=4] {'zb','za'}, dimensions={0}, use_global_device_ids=true | all-gather | bytes 921600 | tf_op jit(solution)/shard_map/all_gather | solution.py:280
  39.3 5.5 %collective-permute-start.1 = (bf16[8,400,128]{2,1,0:T(8,128)(2,1)}, bf16[8,400,128]{2,1,0:T(8,128)(2,1)}, u32[]{:S(2)}, u32[]{:S(2)}) collective-permute-start(bf16[8,400,128]{2,1,0:T(8,128)(2,1)} %bitcast.5.own_ref), channel_id=1, source_target_pairs={{0,4},{4,0},{1,5},{5,1},{2,6},{6,2},{3,7},{7,3},{8,12},{12,8},{9,1... | collective-permute-start | bytes 2457608 | tf_op jit(solution)/shard_map/ppermute | solution.py:254
  44.8 2.3 collective-permute-done.1.far_ref
  47.1 2.6 %project.1 = f32[4,136,256]{2,1,0:T(8,128)S(1)} custom-call(s32[1]{0:T(128)} %bitcast.core, bf16[4,128,3072]{2,1,0:T(8,128)(2,1)S(1)} %all-to-all-done.rows_ref, bf16[8,400,128]{2,1,0:T(8,128)(2,1)} %bitcast.5.own_ref, bf16[8,400,128]{2,1,0:T(8,128)(2,1)} %collective-permute-done.1.far_ref), custom_call_target="tpu_custom_call" | custom-call | flops 805306368 | bytes 8388608 | tf_op jit(solution)/shard_map/project/pallas_call | solution.py:225
  49.8 0.8 copy-done
  50.6 4.5 %all-to-all-start.1 = ((f32[4,136,256]{2,1,0:T(8,128)}), f32[4,136,256]{2,1,0:T(8,128)}, u32[]{:S(2)}, u32[]{:S(2)}) async-start(f32[4,136,256]{2,1,0:T(8,128)} %copy-done), calls=%async_computation.1 | async-start | bytes 1114112 | tf_op jit(solution)/shard_map/all_to_all | solution.py:295
  55.1 8.7 %all-to-all-done.1 = f32[4,136,256]{2,1,0:T(8,128)} async-done(((f32[4,136,256]{2,1,0:T(8,128)}), f32[4,136,256]{2,1,0:T(8,128)}, u32[]{:S(2)}, u32[]{:S(2)}) %all-to-all-start.1) | async-done | bytes 557088 | tf_op jit(solution)/shard_map/all_to_all | solution.py:295
  63.7 1.1 slice_reduce_fusion
  64.8 2.5 %collective-permute-start.2 = (bf16[128,256]{1,0:T(8,128)(2,1)S(1)}, bf16[128,256]{1,0:T(8,128)(2,1)S(1)}, u32[]{:S(2)}, u32[]{:S(2)}) collective-permute-start(bf16[128,256]{1,0:T(8,128)(2,1)S(1)} %slice_reduce_fusion), channel_id=1, source_target_pairs={{0,128},{64,192},{1,129},{65,193},{2,130},{66,194},{3,131},{67,195... | collective-permute-start | bytes 196616 | tf_op jit(solution)/shard_map/ppermute | solution.py:305
  67.3 2.8 %collective-permute-start.3 = (bf16[128,256]{1,0:T(8,128)(2,1)S(1)}, bf16[128,256]{1,0:T(8,128)(2,1)S(1)}, u32[]{:S(2)}, u32[]{:S(2)}) collective-permute-start(bf16[128,256]{1,0:T(8,128)(2,1)S(1)} %slice_reduce_fusion), channel_id=1, source_target_pairs={{0,64},{64,128},{128,192},{1,65},{65,129},{129,193},{2,66},{66,130... | collective-permute-start | bytes 196616 | tf_op jit(solution)/shard_map/ppermute | solution.py:304
  70.2 0.1 broadcast_select_fusion
  70.3 1.3 collective-permute-done.3
  71.6 1.1 pad_maximum_fusion
  72.7 6.6 %all-to-all-start.2 = ((bf16[8,2,128,256]{3,2,1,0:T(8,128)(2,1)}), bf16[8,2,128,256]{3,2,1,0:T(8,128)(2,1)}, u32[]{:S(2)}, u32[]{:S(2)}) async-start(bf16[8,2,128,256]{3,2,1,0:T(8,128)(2,1)} %pad_maximum_fusion), calls=%async_computation.2 | async-start | bytes 2097152 | tf_op jit(solution)/shard_map/all_to_all | solution.py:314
  79.3 0.7 collective-permute-start
  80.0 25.0 %all-to-all-done.2.own = bf16[8,2,128,256]{3,2,1,0:T(8,128)(2,1)} async-done(((bf16[8,2,128,256]{3,2,1,0:T(8,128)(2,1)}), bf16[8,2,128,256]{3,2,1,0:T(8,128)(2,1)}, u32[]{:S(2)}, u32[]{:S(2)}) %all-to-all-start.2) | async-done | bytes 1048608 | tf_op jit(solution)/shard_map/all_to_all | solution.py:314
  105.0 4.1 %collective-permute-start.4 = (bf16[8,2,128,256]{3,2,1,0:T(8,128)(2,1)}, bf16[8,2,128,256]{3,2,1,0:T(8,128)(2,1)}, u32[]{:S(2)}, u32[]{:S(2)}) collective-permute-start(bf16[8,2,128,256]{3,2,1,0:T(8,128)(2,1)} %all-to-all-done.2.own), channel_id=1, source_target_pairs={{0,4},{4,0},{1,5},{5,1},{2,6},{6,2},{3,7},{7,3},{8,12},{12,8},{9,1... | collective-permute-start | bytes 3145736 | tf_op jit(solution)/shard_map/ppermute | solution.py:254
  109.1 0.8 slice_reduce_fusion.1
  109.9 0.1 add_subtract_fusion
  110.1 1.0 broadcast_in_dim.39
  111.0 4.2 %all-to-all-start.3 = ((bf16[8,192,256]{2,1,0:T(8,128)(2,1)}), bf16[8,192,256]{2,1,0:T(8,128)(2,1)}, u32[]{:S(2)}, u32[]{:S(2)}) async-start(bf16[8,192,256]{2,1,0:T(8,128)(2,1)} %broadcast_in_dim.39), calls=%async_computation.3 | async-start | bytes 1572864 | tf_op jit(solution)/shard_map/all_to_all | solution.py:317
  115.3 1.0 copy-done.6
  116.3 1.0 copy-done.7
  117.3 1.0 copy-done.8
  118.3 24.0 %attend.1 = (bf16[8,2,128,256]{3,2,1,0:T(8,128)(2,1)S(1)}, bf16[8,2,128,256]{3,2,1,0:T(8,128)(2,1)S(1)}, bf16[128,256]{1,0:T(8,128)(2,1)S(1)}, bf16[128,256]{1,0:T(8,128)(2,1)S(1)}) custom-call(s32[5]{0:T(128)S(1)} %pad_add_fusion.2.place, bf16[8,2,128,256]{3,2,1,0:T(8,128)(2,1)} %all-to-all-done.2.own, bf16[8,2,128,256]{3,2,1,0:T(8,128)(2,1)} %collective-permute-done.4.far, ...), custom_call_target="tpu_custom_call" | custom-call | flops 6845104128 | bytes 8388608 | tf_op jit(solution)/shard_map/attend/pallas_call | solution.py:127
  142.3 0.8 collective-permute-start.6
  143.1 2.3 collective-permute-done.6
  145.4 1.3 add_convert_fusion
  146.7 6.8 %all-to-all-start.4 = ((bf16[8,2,128,256]{3,2,1,0:T(8,128)(2,1)}), bf16[8,2,128,256]{3,2,1,0:T(8,128)(2,1)}, u32[]{:S(2)}, u32[]{:S(2)}) async-start(bf16[8,2,128,256]{3,2,1,0:T(8,128)(2,1)} %add_convert_fusion), calls=%async_computation.4 | async-start | bytes 2097152 | tf_op jit(solution)/shard_map/all_to_all | solution.py:326
  153.4 1.9 collective-permute-start.7
  155.4 0.8 collective-permute-start.8
  156.1 17.3 %collective-permute-done.7.refs_1_ = bf16[8,192,256]{2,1,0:T(8,128)(2,1)S(1)} collective-permute-done((bf16[8,192,256]{2,1,0:T(8,128)(2,1)}, bf16[8,192,256]{2,1,0:T(8,128)(2,1)S(1)}, u32[]{:S(2)}, u32[]{:S(2)}) %collective-permute-start.7) | collective-permute-done | bytes 786464 | tf_op jit(solution)/shard_map/ppermute | solution.py:329
  173.4 0.9 copy-done.1
  174.3 0.8 collective-permute-start.9
  175.1 0.9 copy-done.4
  176.0 2.1 collective-permute-start.10
  178.1 2.0 collective-permute-start.11
  180.2 0.8 collective-permute-done.11
  181.1 3.8 %collective-permute-done.9.refs_2_ = bf16[4,192,256]{2,1,0:T(8,128)(2,1)} collective-permute-done((bf16[4,192,256]{2,1,0:T(8,128)(2,1)S(1)}, bf16[4,192,256]{2,1,0:T(8,128)(2,1)}, u32[]{:S(2)}, u32[]{:S(2)}) %collective-permute-start.9) | collective-permute-done | bytes 393248 | tf_op jit(solution)/shard_map/ppermute | solution.py:329
  184.9 0.2 collective-permute-done.10.refs_3_
  185.1 1.5 window_sums.1
  186.6 11.4 %all-gather.1 = bf16[12,128,256]{2,1,0:T(8,128)(2,1)S(1)} all-gather(bf16[3,128,256]{2,1,0:T(8,128)(2,1)S(1)} %window_sums.1), channel_id=3, replica_groups=mesh['y'=4,'zb'=4,'za'=2,'c'=2,'x'=4] {'y'}, dimensions={0}, use_global_device_ids=true | all-gather | bytes 983040 | tf_op jit(solution)/shard_map/all_gather | solution.py:342
  198.0 1.7 weight_terms.1
  199.7 5.8 %collective-permute-start.12 = (bf16[8,192,256]{2,1,0:T(8,128)(2,1)S(1)}, bf16[8,192,256]{2,1,0:T(8,128)(2,1)S(1)}, u32[]{:S(2)}, u32[]{:S(2)}) collective-permute-start(bf16[8,192,256]{2,1,0:T(8,128)(2,1)S(1)} %get-tuple-element.50), channel_id=1, source_target_pairs={{0,4},{4,0},{1,5},{5,1},{2,6},{6,2},{3,7},{7,3},{8,12},{12,8},{9,1... | collective-permute-start | bytes 2359304 | tf_op jit(solution)/shard_map/ppermute | solution.py:254
  205.4 1.9 collective-permute-done.12
  207.3 1.1 add_convert_fusion.1
  208.4 6.2 %all-to-all-start.5 = ((bf16[8,192,256]{2,1,0:T(8,128)(2,1)}), bf16[8,192,256]{2,1,0:T(8,128)(2,1)}, u32[]{:S(2)}, u32[]{:S(2)}) async-start(bf16[8,192,256]{2,1,0:T(8,128)(2,1)} %add_convert_fusion.1), calls=%async_computation.5 | async-start | bytes 1572864 | tf_op jit(solution)/shard_map/all_to_all | solution.py:353
  214.7 0.7 collective-permute-start.13
  215.3 0.1 collective-permute-start.14
  215.4 0.4 collective-permute-start.17
  215.8 0.1 collective-permute-start.15
  215.9 0.4 collective-permute-start.16
  216.3 2.3 collective-permute-done.15.refs_7_
  218.6 1.1 collective-permute-done.16.refs_8_
  219.8 0.8 collective-permute-done.17.refs_9_
  220.6 10.9 %all-gather.2 = bf16[512,256]{1,0:T(8,128)(2,1)S(1)} all-gather(bf16[128,256]{1,0:T(8,128)(2,1)S(1)} %get-tuple-element.57), channel_id=4, replica_groups=mesh['y'=4,'zb'=4,'za'=2,'c'=2,'x'=4] {'x'}, dimensions={0}, use_global_device_ids=true | all-gather | bytes 327680 | tf_op jit(solution)/shard_map/all_gather | solution.py:356
  231.5 4.6 %input_terms.1 = f32[128,3072]{1,0:T(8,128)} custom-call(s32[2]{0:T(128)S(1)} %pad_add_fusion.place, bf16[4,128,256]{2,1,0:T(8,128)(2,1)S(1)} %bitcast.10, bf16[8,192,256]{2,1,0:T(8,128)(2,1)} %all-to-all-done.3.refs_0_, bf16[8,192,256]{2,1,0:T(8,128)(2,1)S(1)} %copy-done.3, bf16[4,192,256]{2,1,0:T(8,128)(2,1)} %collective-permute-done.9.refs_2_, ...), custom_call_target="tpu_custom_call" | custom-call | flops 805306368 | bytes 8388608 | tf_op jit(solution)/shard_map/input_terms/pallas_call | solution.py:225
  236.1 2.2 all-to-all-done.5
  238.3 1.3 convert_reduce_fusion
  239.6 0.7 fusion.5
  (41 shorter events, 0.5 us)
Async XLA Ops:
  4.8 5.2 %copy-start.11 = (s32[128]{0:T(128)S(1)}, s32[128]{0:T(128)}, u32[]{:S(2)}) copy-start(s32[128]{0:T(128)} %param.15) | copy-start | bytes 1540
  4.8 7.2 %copy-start.9 = (bf16[192,128]{1,0:T(8,128)(2,1)S(1)}, bf16[192,128]{1,0:T(8,128)(2,1)}, u32[]{:S(2)}) copy-start(bf16[192,128]{1,0:T(8,128)(2,1)} %param.11) | copy-start | bytes 147460
  4.8 7.2 %copy-start.10 = (bf16[192,128]{1,0:T(8,128)(2,1)S(1)}, bf16[192,128]{1,0:T(8,128)(2,1)}, u32[]{:S(2)}) copy-start(bf16[192,128]{1,0:T(8,128)(2,1)} %param.10) | copy-start | bytes 147460
  4.8 42.3 %all-to-all-start = ((bf16[4,128,3072]{2,1,0:T(8,128)(2,1)}), bf16[4,128,3072]{2,1,0:T(8,128)(2,1)S(1)}, u32[]{:S(2)}, u32[]{:S(2)}) async-start(bf16[4,128,3072]{2,1,0:T(8,128)(2,1)} %split_columns.1), calls=%async_computation | async-start | bytes 6291456 | tf_op jit(solution)/shard_map/all_to_all | solution.py:270
  39.3 7.8 %collective-permute-start.1 = (bf16[8,400,128]{2,1,0:T(8,128)(2,1)}, bf16[8,400,128]{2,1,0:T(8,128)(2,1)}, u32[]{:S(2)}, u32[]{:S(2)}) collective-permute-start(bf16[8,400,128]{2,1,0:T(8,128)(2,1)} %bitcast.5.own_ref), channel_id=1, source_target_pairs={{0,4},{4,0},{1,5},{5,1},{2,6},{6,2},{3,7},{7,3},{8,12},{12,8},{9,1... | collective-permute-start | bytes 2457608 | tf_op jit(solution)/shard_map/ppermute | solution.py:254
  49.7 0.8 copy-start
  50.6 13.2 %all-to-all-start.1 = ((f32[4,136,256]{2,1,0:T(8,128)}), f32[4,136,256]{2,1,0:T(8,128)}, u32[]{:S(2)}, u32[]{:S(2)}) async-start(f32[4,136,256]{2,1,0:T(8,128)} %copy-done), calls=%async_computation.1 | async-start | bytes 1114112 | tf_op jit(solution)/shard_map/all_to_all | solution.py:295
  64.8 5.3 %collective-permute-start.2 = (bf16[128,256]{1,0:T(8,128)(2,1)S(1)}, bf16[128,256]{1,0:T(8,128)(2,1)S(1)}, u32[]{:S(2)}, u32[]{:S(2)}) collective-permute-start(bf16[128,256]{1,0:T(8,128)(2,1)S(1)} %slice_reduce_fusion), channel_id=1, source_target_pairs={{0,128},{64,192},{1,129},{65,193},{2,130},{66,194},{3,131},{67,195... | collective-permute-start | bytes 196616 | tf_op jit(solution)/shard_map/ppermute | solution.py:305
  67.3 4.2 %collective-permute-start.3 = (bf16[128,256]{1,0:T(8,128)(2,1)S(1)}, bf16[128,256]{1,0:T(8,128)(2,1)S(1)}, u32[]{:S(2)}, u32[]{:S(2)}) collective-permute-start(bf16[128,256]{1,0:T(8,128)(2,1)S(1)} %slice_reduce_fusion), channel_id=1, source_target_pairs={{0,64},{64,128},{128,192},{1,65},{65,129},{129,193},{2,66},{66,130... | collective-permute-start | bytes 196616 | tf_op jit(solution)/shard_map/ppermute | solution.py:304
  72.7 32.3 %all-to-all-start.2 = ((bf16[8,2,128,256]{3,2,1,0:T(8,128)(2,1)}), bf16[8,2,128,256]{3,2,1,0:T(8,128)(2,1)}, u32[]{:S(2)}, u32[]{:S(2)}) async-start(bf16[8,2,128,256]{3,2,1,0:T(8,128)(2,1)} %pad_maximum_fusion), calls=%async_computation.2 | async-start | bytes 2097152 | tf_op jit(solution)/shard_map/all_to_all | solution.py:314
  79.3 0.7 collective-permute-start
  105.0 10.3 %collective-permute-start.4 = (bf16[8,2,128,256]{3,2,1,0:T(8,128)(2,1)}, bf16[8,2,128,256]{3,2,1,0:T(8,128)(2,1)}, u32[]{:S(2)}, u32[]{:S(2)}) collective-permute-start(bf16[8,2,128,256]{3,2,1,0:T(8,128)(2,1)} %all-to-all-done.2.own), channel_id=1, source_target_pairs={{0,4},{4,0},{1,5},{5,1},{2,6},{6,2},{3,7},{7,3},{8,12},{12,8},{9,1... | collective-permute-start | bytes 3145736 | tf_op jit(solution)/shard_map/ppermute | solution.py:254
  110.0 5.3 %collective-permute-start.5 = (bf16[128,256]{1,0:T(8,128)(2,1)S(1)}, bf16[128,256]{1,0:T(8,128)(2,1)S(1)}, u32[]{:S(2)}, u32[]{:S(2)}) collective-permute-start(bf16[128,256]{1,0:T(8,128)(2,1)S(1)} %collective-permute-done.2.own_back), channel_id=1, source_target_pairs={{0,4},{4,0},{1,5},{5,1},{2,6},{6,2},{3,7},{7,3},{8,12},{12,8},{9,1... | collective-permute-start | bytes 196616 | tf_op jit(solution)/shard_map/ppermute | solution.py:254
  111.0 35.6 %all-to-all-start.3 = ((bf16[8,192,256]{2,1,0:T(8,128)(2,1)}), bf16[8,192,256]{2,1,0:T(8,128)(2,1)}, u32[]{:S(2)}, u32[]{:S(2)}) async-start(bf16[8,192,256]{2,1,0:T(8,128)(2,1)} %broadcast_in_dim.39), calls=%async_computation.3 | async-start | bytes 1572864 | tf_op jit(solution)/shard_map/all_to_all | solution.py:317
  115.3 1.0 copy-start.6
  116.3 1.0 copy-start.7
  117.3 1.0 copy-start.8
  142.3 3.1 %collective-permute-start.6 = (bf16[8,2,128,256]{3,2,1,0:T(8,128)(2,1)S(1)}, bf16[8,2,128,256]{3,2,1,0:T(8,128)(2,1)S(1)}, u32[]{:S(2)}, u32[]{:S(2)}) collective-permute-start(bf16[8,2,128,256]{3,2,1,0:T(8,128)(2,1)S(1)} %get-tuple-element.43), channel_id=1, source_target_pairs={{0,4},{4,0},{1,5},{5,1},{2,6},{6,2},{3,7},{7,3},{8,12},{12,8},{9,1... | collective-permute-start | bytes 3145736 | tf_op jit(solution)/shard_map/ppermute | solution.py:254
  146.7 38.5 %all-to-all-start.4 = ((bf16[8,2,128,256]{3,2,1,0:T(8,128)(2,1)}), bf16[8,2,128,256]{3,2,1,0:T(8,128)(2,1)}, u32[]{:S(2)}, u32[]{:S(2)}) async-start(bf16[8,2,128,256]{3,2,1,0:T(8,128)(2,1)} %add_convert_fusion), calls=%async_computation.4 | async-start | bytes 2097152 | tf_op jit(solution)/shard_map/all_to_all | solution.py:326
  153.4 20.0 %collective-permute-start.7 = (bf16[8,192,256]{2,1,0:T(8,128)(2,1)}, bf16[8,192,256]{2,1,0:T(8,128)(2,1)S(1)}, u32[]{:S(2)}, u32[]{:S(2)}) collective-permute-start(bf16[8,192,256]{2,1,0:T(8,128)(2,1)} %all-to-all-done.3.refs_0_), channel_id=1, source_target_pairs={{0,64},{64,128},{128,192},{192,0},{1,65},{65,129},{129,193},{193,1... | collective-permute-start | bytes 2359304 | tf_op jit(solution)/shard_map/ppermute | solution.py:329
  155.4 19.7 %collective-permute-start.8 = (bf16[8,192,256]{2,1,0:T(8,128)(2,1)}, bf16[8,192,256]{2,1,0:T(8,128)(2,1)S(1)}, u32[]{:S(2)}, u32[]{:S(2)}) collective-permute-start(bf16[8,192,256]{2,1,0:T(8,128)(2,1)} %all-to-all-done.3.refs_0_), channel_id=1, source_target_pairs={{0,192},{64,0},{128,64},{192,128},{1,193},{65,1},{129,65},{193,129... | collective-permute-start | bytes 2359304 | tf_op jit(solution)/shard_map/ppermute | solution.py:329
  173.4 0.9 copy-start.1
  174.3 10.6 %collective-permute-start.9 = (bf16[4,192,256]{2,1,0:T(8,128)(2,1)S(1)}, bf16[4,192,256]{2,1,0:T(8,128)(2,1)}, u32[]{:S(2)}, u32[]{:S(2)}) collective-permute-start(bf16[4,192,256]{2,1,0:T(8,128)(2,1)S(1)} %slice.46), channel_id=1, source_target_pairs={{0,64},{64,128},{128,192},{192,0},{1,65},{65,129},{129,193},{193,1... | collective-permute-start | bytes 1179656 | tf_op jit(solution)/shard_map/ppermute | solution.py:329
  175.1 0.9 copy-start.4
  176.0 9.1 %collective-permute-start.10 = (bf16[4,192,256]{2,1,0:T(8,128)(2,1)S(1)}, bf16[4,192,256]{2,1,0:T(8,128)(2,1)}, u32[]{:S(2)}, u32[]{:S(2)}) collective-permute-start(bf16[4,192,256]{2,1,0:T(8,128)(2,1)S(1)} %slice.47), channel_id=1, source_target_pairs={{0,192},{64,0},{128,64},{192,128},{1,193},{65,1},{129,65},{193,129... | collective-permute-start | bytes 1179656 | tf_op jit(solution)/shard_map/ppermute | solution.py:329
  178.1 2.9 %collective-permute-start.11 = (bf16[128,256]{1,0:T(8,128)(2,1)S(1)}, bf16[128,256]{1,0:T(8,128)(2,1)S(1)}, u32[]{:S(2)}, u32[]{:S(2)}) collective-permute-start(bf16[128,256]{1,0:T(8,128)(2,1)S(1)} %get-tuple-element.48), channel_id=1, source_target_pairs={{0,4},{4,0},{1,5},{5,1},{2,6},{6,2},{3,7},{7,3},{8,12},{12,8},{9,1... | collective-permute-start | bytes 196616 | tf_op jit(solution)/shard_map/ppermute | solution.py:254
  199.7 7.7 %collective-permute-start.12 = (bf16[8,192,256]{2,1,0:T(8,128)(2,1)S(1)}, bf16[8,192,256]{2,1,0:T(8,128)(2,1)S(1)}, u32[]{:S(2)}, u32[]{:S(2)}) collective-permute-start(bf16[8,192,256]{2,1,0:T(8,128)(2,1)S(1)} %get-tuple-element.50), channel_id=1, source_target_pairs={{0,4},{4,0},{1,5},{5,1},{2,6},{6,2},{3,7},{7,3},{8,12},{12,8},{9,1... | collective-permute-start | bytes 2359304 | tf_op jit(solution)/shard_map/ppermute | solution.py:254
  207.3 8.0 %copy-start.2 = (bf16[8,192,256]{2,1,0:T(8,128)(2,1)S(1)}, bf16[8,192,256]{2,1,0:T(8,128)(2,1)}, u32[]{:S(2)}) copy-start(bf16[8,192,256]{2,1,0:T(8,128)(2,1)} %copy-done.1) | copy-start | bytes 2359300
  207.3 8.1 %copy-start.5 = (bf16[8,192,256]{2,1,0:T(8,128)(2,1)S(1)}, bf16[8,192,256]{2,1,0:T(8,128)(2,1)}, u32[]{:S(2)}) copy-start(bf16[8,192,256]{2,1,0:T(8,128)(2,1)} %copy-done.4) | copy-start | bytes 2359300
  207.3 24.2 %copy-start.3 = (bf16[8,192,256]{2,1,0:T(8,128)(2,1)S(1)}, bf16[8,192,256]{2,1,0:T(8,128)(2,1)}, u32[]{:S(2)}) copy-start(bf16[8,192,256]{2,1,0:T(8,128)(2,1)} %copy-done.1) | copy-start | bytes 2359300
  208.4 29.9 %all-to-all-start.5 = ((bf16[8,192,256]{2,1,0:T(8,128)(2,1)}), bf16[8,192,256]{2,1,0:T(8,128)(2,1)}, u32[]{:S(2)}, u32[]{:S(2)}) async-start(bf16[8,192,256]{2,1,0:T(8,128)(2,1)} %add_convert_fusion.1), calls=%async_computation.5 | async-start | bytes 1572864 | tf_op jit(solution)/shard_map/all_to_all | solution.py:353
  214.7 5.1 %collective-permute-start.13 = (bf16[8,192,256]{2,1,0:T(8,128)(2,1)}, bf16[8,192,256]{2,1,0:T(8,128)(2,1)S(1)}, u32[]{:S(2)}, u32[]{:S(2)}) collective-permute-start(bf16[8,192,256]{2,1,0:T(8,128)(2,1)} %all-to-all-done.3.refs_0_), channel_id=1, source_target_pairs={{0,4},{4,0},{1,5},{5,1},{2,6},{6,2},{3,7},{7,3},{8,12},{12,8},{9,1... | collective-permute-start | bytes 2359304 | tf_op jit(solution)/shard_map/ppermute | solution.py:254
  215.3 4.4 %collective-permute-start.14 = (bf16[8,192,256]{2,1,0:T(8,128)(2,1)S(1)}, bf16[8,192,256]{2,1,0:T(8,128)(2,1)S(1)}, u32[]{:S(2)}, u32[]{:S(2)}) collective-permute-start(bf16[8,192,256]{2,1,0:T(8,128)(2,1)S(1)} %copy-done.2), channel_id=1, source_target_pairs={{0,4},{4,0},{1,5},{5,1},{2,6},{6,2},{3,7},{7,3},{8,12},{12,8},{9,1... | collective-permute-start | bytes 2359304 | tf_op jit(solution)/shard_map/ppermute | solution.py:254
  215.4 5.2 %collective-permute-start.17 = (bf16[8,192,256]{2,1,0:T(8,128)(2,1)S(1)}, bf16[8,192,256]{2,1,0:T(8,128)(2,1)S(1)}, u32[]{:S(2)}, u32[]{:S(2)}) collective-permute-start(bf16[8,192,256]{2,1,0:T(8,128)(2,1)S(1)} %copy-done.5), channel_id=1, source_target_pairs={{0,4},{4,0},{1,5},{5,1},{2,6},{6,2},{3,7},{7,3},{8,12},{12,8},{9,1... | collective-permute-start | bytes 2359304 | tf_op jit(solution)/shard_map/ppermute | solution.py:254
  215.8 2.8 %collective-permute-start.15 = (bf16[4,192,256]{2,1,0:T(8,128)(2,1)}, bf16[4,192,256]{2,1,0:T(8,128)(2,1)S(1)}, u32[]{:S(2)}, u32[]{:S(2)}) collective-permute-start(bf16[4,192,256]{2,1,0:T(8,128)(2,1)} %collective-permute-done.9.refs_2_), channel_id=1, source_target_pairs={{0,4},{4,0},{1,5},{5,1},{2,6},{6,2},{3,7},{7,3},{8,12},{12,8},{9,1... | collective-permute-start | bytes 1179656 | tf_op jit(solution)/shard_map/ppermute | solution.py:254
  215.9 3.8 %collective-permute-start.16 = (bf16[4,192,256]{2,1,0:T(8,128)(2,1)}, bf16[4,192,256]{2,1,0:T(8,128)(2,1)S(1)}, u32[]{:S(2)}, u32[]{:S(2)}) collective-permute-start(bf16[4,192,256]{2,1,0:T(8,128)(2,1)} %collective-permute-done.10.refs_3_), channel_id=1, source_target_pairs={{0,4},{4,0},{1,5},{5,1},{2,6},{6,2},{3,7},{7,3},{8,12},{12,8},{9,1... | collective-permute-start | bytes 1179656 | tf_op jit(solution)/shard_map/ppermute | solution.py:254

commit v4 on v3

--- a/solution.py
+++ b/solution.py
@@ -329,17 +329,17 @@
         return lax.ppermute(a, "y", [(i, (i + k) % ys) for i in range(ys)])
 
     w_1, w_3 = along(w_z, 1), along(w_z, 3)
+    parts, w_z, w_1, w_3 = lax.optimization_barrier((parts, w_z, w_1, w_3))
     half = RING // 2
     w_2 = along(w_1[:half], 1), along(w_3[half:], 3)
-    parts, w_z, w_1, w_3, *w_2 = lax.optimization_barrier((parts, w_z, w_1, w_3, *w_2))
-    w_own = [w_z, w_1, *w_2, w_3]
-    w_far = [swap(one) for one in w_own]
+    f_z, f_1, f_3 = swap(w_z), swap(w_1), swap(w_3)
     sums = kernel_call(
         window_sums,
         shape((3, ROWS, 2 * HD), bf16),
         (place, parts, mine_back),
     )
     sums = lax.all_gather(sums, "y", axis=0)
+    sums, *w_2 = lax.optimization_barrier((sums, *w_2))
 
     dims = (RING, depth, 2 * HD)
     near, far, grad_terms = kernel_call(
@@ -352,7 +352,9 @@
     summed = (near + swap(far).astype(f32)).astype(bf16)
     parts = lax.all_to_all(summed, ring, 0, 0)
 
+    w_far = [f_z, f_1, *(swap(one) for one in w_2), f_3]
     tied, *w_far = lax.optimization_barrier((grad_terms, *w_far))
+    w_own = [w_z, w_1, *w_2, w_3]
     terms_x = lax.all_gather(tied, "x", axis=0)
     input_grad = kernel_call(
         input_terms,

time: 241 us -> 246 us (1.021)
  starting transfers between devices: 64.8 us -> 58.4 us
  blocking collectives: 49.5 us -> 52.7 us
  local copies, waits for them, and re-layouts: 7.31 us -> 10.5 us
  waiting for transfers between devices: 70.2 us -> 73.2 us
    all_to_all x1, waiting for transfers between devices: 0.01 us -> 9.05 us  [body(): parts = lax.all_to_all(mine, ring, 0, 0)]
    ppermute x4, waiting for transfers between devices: 21.3 us -> 17.2 us  [along(): return lax.ppermute(a, 'y', [(i, (i + k) % ys) for i in range(ys)])]
    all_gather x1, blocking collectives: 11.4 us -> 14.5 us  [body(): sums = lax.all_gather(sums, 'y', axis=0)]
    ppermute x11, starting transfers between devices: 19.9 us -> 16.9 us  [swap(): return lax.ppermute(a, axis, [(0, 1), (1, 0)])]
    unnamed x24 -> x26, local copies, waits for them, and re-layouts: 5.58 us -> 6.79 us
  transfers between devices with their start and end apart: 24 -> 24, of which waited for: 14 -> 14; matrix products, arithmetic and copies ran while one was open for 2% -> 3% of each run, Pallas kernels for 12% -> 13%
where the time goes in v4:
time: 246 us; the launch traced here: 245 us
  waiting for transfers between devices  73.2 us (30%)
  starting transfers between devices  58.4 us (24%)
  blocking collectives  52.7 us (21%)
  Pallas kernels  39.5 us (16%)
  local copies, waits for them, and re-layouts  10.5 us (4%)
  other arithmetic  9.88 us (4%)
    all_gather x1, blocking collectives, body(): lax.all_gather(jnp.concatenate((w_key, w_value, counts), 0), ('zb', 'za')...  27.3 us
    all_to_all x1, waiting for transfers between devices, body(): own = lax.all_to_all(send, ring, 0, 0)  25 us
    pallas_call x1, Pallas kernels, attention(): pl.pallas_call(attend, out_shape=(out, out, back, back), in_specs=[pl.Blo...  24.6 us
    ppermute x4, waiting for transfers between devices, along(): return lax.ppermute(a, 'y', [(i, (i + k) % ys) for i in range(ys)])  17.2 us
    ppermute x11, starting transfers between devices, swap(): return lax.ppermute(a, axis, [(0, 1), (1, 0)])  16.9 us
    all_gather x1, blocking collectives, body(): sums = lax.all_gather(sums, 'y', axis=0)  14.5 us
    ppermute x11, waiting for transfers between devices, swap(): return lax.ppermute(a, axis, [(0, 1), (1, 0)])  11 us
    all_gather x1, blocking collectives, body(): terms_x = lax.all_gather(tied, 'x', axis=0)  10.9 us
  transfers between devices with their start and end apart: 24, of which 14 were waited for; matrix products, arithmetic and copies ran while one was open for 3% of the time, Pallas kernels for 13%

profile of v4, /device:TPU:1, one launch (start us, length us, event | category | flops | bytes accessed | tf_op | source)
XLA Modules:
  0.0 245.0 jit_solution(823124586291001428)
XLA Ops:
  0.6 4.2 %split_columns.1 = bf16[4,128,3072]{2,1,0:T(8,128)(2,1)} custom-call(bf16[128,12288]{1,0:T(8,128)(2,1)} %src.1), custom_call_target="tpu_custom_call" | custom-call | tf_op jit(solution)/shard_map/split_columns/pallas_call | solution.py:243
  4.8 5.2 %all-to-all-start = ((bf16[4,128,3072]{2,1,0:T(8,128)(2,1)}), bf16[4,128,3072]{2,1,0:T(8,128)(2,1)S(1)}, u32[]{:S(2)}, u32[]{:S(2)}) async-start(bf16[4,128,3072]{2,1,0:T(8,128)(2,1)} %split_columns.1), calls=%async_computation | async-start | bytes 6291456 | tf_op jit(solution)/shard_map/all_to_all | solution.py:270
  10.0 0.6 fusion.2
  10.6 1.4 fusion.4
  12.0 27.3 %all-gather = bf16[3200,128]{1,0:T(8,128)(2,1)} all-gather(bf16[400,128]{1,0:T(8,128)(2,1)S(1)} %fusion.1), channel_id=2, replica_groups=mesh['y'=4,'zb'=4,'za'=2,'c'=2,'x'=4] {'zb','za'}, dimensions={0}, use_global_device_ids=true | all-gather | bytes 921600 | tf_op jit(solution)/shard_map/all_gather | solution.py:280
  39.3 5.5 %collective-permute-start.1 = (bf16[8,400,128]{2,1,0:T(8,128)(2,1)}, bf16[8,400,128]{2,1,0:T(8,128)(2,1)}, u32[]{:S(2)}, u32[]{:S(2)}) collective-permute-start(bf16[8,400,128]{2,1,0:T(8,128)(2,1)} %bitcast.5.own_ref), channel_id=1, source_target_pairs={{0,4},{4,0},{1,5},{5,1},{2,6},{6,2},{3,7},{7,3},{8,12},{12,8},{9,1... | collective-permute-start | bytes 2457608 | tf_op jit(solution)/shard_map/ppermute | solution.py:254
  44.8 2.3 collective-permute-done.1.far_ref
  47.1 2.6 %project.1 = f32[4,136,256]{2,1,0:T(8,128)S(1)} custom-call(s32[1]{0:T(128)} %bitcast.core, bf16[4,128,3072]{2,1,0:T(8,128)(2,1)S(1)} %all-to-all-done.rows_ref, bf16[8,400,128]{2,1,0:T(8,128)(2,1)} %bitcast.5.own_ref, bf16[8,400,128]{2,1,0:T(8,128)(2,1)} %collective-permute-done.1.far_ref), custom_call_target="tpu_custom_call" | custom-call | flops 805306368 | bytes 8388608 | tf_op jit(solution)/shard_map/project/pallas_call | solution.py:225
  49.8 0.8 copy-done
  50.6 4.5 %all-to-all-start.1 = ((f32[4,136,256]{2,1,0:T(8,128)}), f32[4,136,256]{2,1,0:T(8,128)}, u32[]{:S(2)}, u32[]{:S(2)}) async-start(f32[4,136,256]{2,1,0:T(8,128)} %copy-done), calls=%async_computation.1 | async-start | bytes 1114112 | tf_op jit(solution)/shard_map/all_to_all | solution.py:295
  55.1 8.7 %all-to-all-done.1 = f32[4,136,256]{2,1,0:T(8,128)} async-done(((f32[4,136,256]{2,1,0:T(8,128)}), f32[4,136,256]{2,1,0:T(8,128)}, u32[]{:S(2)}, u32[]{:S(2)}) %all-to-all-start.1) | async-done | bytes 557088 | tf_op jit(solution)/shard_map/all_to_all | solution.py:295
  63.8 1.1 slice_reduce_fusion
  64.8 2.5 %collective-permute-start.2 = (bf16[128,256]{1,0:T(8,128)(2,1)S(1)}, bf16[128,256]{1,0:T(8,128)(2,1)S(1)}, u32[]{:S(2)}, u32[]{:S(2)}) collective-permute-start(bf16[128,256]{1,0:T(8,128)(2,1)S(1)} %slice_reduce_fusion), channel_id=1, source_target_pairs={{0,128},{64,192},{1,129},{65,193},{2,130},{66,194},{3,131},{67,195... | collective-permute-start | bytes 196616 | tf_op jit(solution)/shard_map/ppermute | solution.py:305
  67.4 2.8 %collective-permute-start.3 = (bf16[128,256]{1,0:T(8,128)(2,1)S(1)}, bf16[128,256]{1,0:T(8,128)(2,1)S(1)}, u32[]{:S(2)}, u32[]{:S(2)}) collective-permute-start(bf16[128,256]{1,0:T(8,128)(2,1)S(1)} %slice_reduce_fusion), channel_id=1, source_target_pairs={{0,64},{64,128},{128,192},{1,65},{65,129},{129,193},{2,66},{66,130... | collective-permute-start | bytes 196616 | tf_op jit(solution)/shard_map/ppermute | solution.py:304
  70.3 1.3 collective-permute-done.3
  71.6 1.1 pad_maximum_fusion
  72.7 6.5 %all-to-all-start.2 = ((bf16[8,2,128,256]{3,2,1,0:T(8,128)(2,1)}), bf16[8,2,128,256]{3,2,1,0:T(8,128)(2,1)}, u32[]{:S(2)}, u32[]{:S(2)}) async-start(bf16[8,2,128,256]{3,2,1,0:T(8,128)(2,1)} %pad_maximum_fusion), calls=%async_computation.2 | async-start | bytes 2097152 | tf_op jit(solution)/shard_map/all_to_all | solution.py:314
  79.3 0.7 collective-permute-start
  80.0 25.0 %all-to-all-done.2.own = bf16[8,2,128,256]{3,2,1,0:T(8,128)(2,1)} async-done(((bf16[8,2,128,256]{3,2,1,0:T(8,128)(2,1)}), bf16[8,2,128,256]{3,2,1,0:T(8,128)(2,1)}, u32[]{:S(2)}, u32[]{:S(2)}) %all-to-all-start.2) | async-done | bytes 1048608 | tf_op jit(solution)/shard_map/all_to_all | solution.py:314
  105.0 4.1 %collective-permute-start.4 = (bf16[8,2,128,256]{3,2,1,0:T(8,128)(2,1)}, bf16[8,2,128,256]{3,2,1,0:T(8,128)(2,1)}, u32[]{:S(2)}, u32[]{:S(2)}) collective-permute-start(bf16[8,2,128,256]{3,2,1,0:T(8,128)(2,1)} %all-to-all-done.2.own), channel_id=1, source_target_pairs={{0,4},{4,0},{1,5},{5,1},{2,6},{6,2},{3,7},{7,3},{8,12},{12,8},{9,1... | collective-permute-start | bytes 3145736 | tf_op jit(solution)/shard_map/ppermute | solution.py:254
  109.1 0.8 slice_reduce_fusion.1
  110.1 1.0 broadcast_in_dim.39
  111.0 4.2 %all-to-all-start.3 = ((bf16[8,192,256]{2,1,0:T(8,128)(2,1)}), bf16[8,192,256]{2,1,0:T(8,128)(2,1)}, u32[]{:S(2)}, u32[]{:S(2)}) async-start(bf16[8,192,256]{2,1,0:T(8,128)(2,1)} %broadcast_in_dim.39), calls=%async_computation.3 | async-start | bytes 1572864 | tf_op jit(solution)/shard_map/all_to_all | solution.py:317
  115.3 1.0 copy-done.7
  116.3 1.0 copy-done.8
  117.3 1.0 copy-done.9
  118.3 24.6 %attend.1 = (bf16[8,2,128,256]{3,2,1,0:T(8,128)(2,1)S(1)}, bf16[8,2,128,256]{3,2,1,0:T(8,128)(2,1)S(1)}, bf16[128,256]{1,0:T(8,128)(2,1)S(1)}, bf16[128,256]{1,0:T(8,128)(2,1)}) custom-call(s32[5]{0:T(128)S(1)} %pad_add_fusion.2.place, bf16[8,2,128,256]{3,2,1,0:T(8,128)(2,1)} %all-to-all-done.2.own, bf16[8,2,128,256]{3,2,1,0:T(8,128)(2,1)} %collective-permute-done.4.far, ...), custom_call_target="tpu_custom_call" | custom-call | flops 6845104128 | bytes 8388608 | tf_op jit(solution)/shard_map/attend/pallas_call | solution.py:127
  142.9 0.6 copy-done.6
  143.5 0.5 collective-permute-start.6
  144.0 2.3 collective-permute-done.6
  146.3 1.3 add_convert_fusion
  147.6 6.8 %all-to-all-start.4 = ((bf16[8,2,128,256]{3,2,1,0:T(8,128)(2,1)}), bf16[8,2,128,256]{3,2,1,0:T(8,128)(2,1)}, u32[]{:S(2)}, u32[]{:S(2)}) async-start(bf16[8,2,128,256]{3,2,1,0:T(8,128)(2,1)} %add_convert_fusion), calls=%async_computation.4 | async-start | bytes 2097152 | tf_op jit(solution)/shard_map/all_to_all | solution.py:326
  154.4 0.7 collective-permute-start.8
  155.0 1.3 collective-permute-start.7
  156.4 0.9 collective-permute-start.9
  157.5 16.4 %collective-permute-done.8.refs_4_ = bf16[8,192,256]{2,1,0:T(8,128)(2,1)} collective-permute-done((bf16[8,192,256]{2,1,0:T(8,128)(2,1)}, bf16[8,192,256]{2,1,0:T(8,128)(2,1)}, u32[]{:S(2)}, u32[]{:S(2)}) %collective-permute-start.8) | collective-permute-done | bytes 786464 | tf_op jit(solution)/shard_map/ppermute | solution.py:329
  173.9 0.8 collective-permute-done.7.refs_1_
  174.7 9.0 %all-to-all-done.4.parts_ref = bf16[8,2,128,256]{3,2,1,0:T(8,128)(2,1)} async-done(((bf16[8,2,128,256]{3,2,1,0:T(8,128)(2,1)}), bf16[8,2,128,256]{3,2,1,0:T(8,128)(2,1)}, u32[]{:S(2)}, u32[]{:S(2)}) %all-to-all-start.4) | async-done | bytes 1048608 | tf_op jit(solution)/shard_map/all_to_all | solution.py:326
  183.7 1.0 slice.40
  184.7 1.0 slice.41
  185.8 0.7 collective-permute-start.11
  186.5 1.3 collective-permute-start.10
  187.9 0.9 convert_add_fusion.back_ref
  188.7 1.5 window_sums.1
  190.3 14.5 %all-gather.1 = bf16[12,128,256]{2,1,0:T(8,128)(2,1)S(1)} all-gather(bf16[3,128,256]{2,1,0:T(8,128)(2,1)S(1)} %window_sums.1), channel_id=3, replica_groups=mesh['y'=4,'zb'=4,'za'=2,'c'=2,'x'=4] {'y'}, dimensions={0}, use_global_device_ids=true | all-gather | bytes 983040 | tf_op jit(solution)/shard_map/all_gather | solution.py:341
  204.8 0.7 copy-done.1
  205.6 1.7 weight_terms.1
  207.3 0.6 copy-done.4
  207.9 4.3 %collective-permute-start.12 = (bf16[8,192,256]{2,1,0:T(8,128)(2,1)S(1)}, bf16[8,192,256]{2,1,0:T(8,128)(2,1)S(1)}, u32[]{:S(2)}, u32[]{:S(2)}) collective-permute-start(bf16[8,192,256]{2,1,0:T(8,128)(2,1)S(1)} %get-tuple-element.54), channel_id=1, source_target_pairs={{0,4},{4,0},{1,5},{5,1},{2,6},{6,2},{3,7},{7,3},{8,12},{12,8},{9,1... | collective-permute-start | bytes 2359304 | tf_op jit(solution)/shard_map/ppermute | solution.py:254
  212.2 1.9 collective-permute-done.12
  214.1 1.1 add_convert_fusion.1
  215.2 4.2 %all-to-all-start.5 = ((bf16[8,192,256]{2,1,0:T(8,128)(2,1)}), bf16[8,192,256]{2,1,0:T(8,128)(2,1)}, u32[]{:S(2)}, u32[]{:S(2)}) async-start(bf16[8,192,256]{2,1,0:T(8,128)(2,1)} %add_convert_fusion.1), calls=%async_computation.5 | async-start | bytes 1572864 | tf_op jit(solution)/shard_map/all_to_all | solution.py:353
  219.4 0.5 collective-permute-start.13
  220.0 0.4 collective-permute-start.17
  220.5 0.4 collective-permute-start.16
  220.9 2.0 collective-permute-done.15.refs_7_
  222.9 1.1 collective-permute-done.16.refs_8_
  224.3 1.1 collective-permute-done.17.refs_9_
  225.4 10.9 %all-gather.2 = bf16[512,256]{1,0:T(8,128)(2,1)S(1)} all-gather(bf16[128,256]{1,0:T(8,128)(2,1)S(1)} %copy-done.5), channel_id=4, replica_groups=mesh['y'=4,'zb'=4,'za'=2,'c'=2,'x'=4] {'x'}, dimensions={0}, use_global_device_ids=true | all-gather | bytes 327680 | tf_op jit(solution)/shard_map/all_gather | solution.py:358
  236.3 1.0 copy-done.3
  237.3 4.9 %input_terms.1 = f32[128,3072]{1,0:T(8,128)} custom-call(s32[2]{0:T(128)S(1)} %pad_add_fusion.place, bf16[4,128,256]{2,1,0:T(8,128)(2,1)S(1)} %bitcast.10, bf16[8,192,256]{2,1,0:T(8,128)(2,1)} %all-to-all-done.3.refs_0_, bf16[8,192,256]{2,1,0:T(8,128)(2,1)} %collective-permute-done.7.refs_1_, bf16[4,192,256]{2,1,0:T(8,128)(2,1)S(1)} %copy-done.3, ...), custom_call_target="tpu_custom_call" | custom-call | flops 805306368 | bytes 8388608 | tf_op jit(solution)/shard_map/input_terms/pallas_call | solution.py:225
  242.1 0.9 all-to-all-done.5
  243.0 1.3 convert_reduce_fusion
  244.3 0.7 fusion.5
  (43 shorter events, 1.1 us)
Async XLA Ops:
  4.8 5.2 %copy-start.12 = (s32[128]{0:T(128)S(1)}, s32[128]{0:T(128)}, u32[]{:S(2)}) copy-start(s32[128]{0:T(128)} %param.15) | copy-start | bytes 1540
  4.8 7.2 %copy-start.10 = (bf16[192,128]{1,0:T(8,128)(2,1)S(1)}, bf16[192,128]{1,0:T(8,128)(2,1)}, u32[]{:S(2)}) copy-start(bf16[192,128]{1,0:T(8,128)(2,1)} %param.11) | copy-start | bytes 147460
  4.8 7.2 %copy-start.11 = (bf16[192,128]{1,0:T(8,128)(2,1)S(1)}, bf16[192,128]{1,0:T(8,128)(2,1)}, u32[]{:S(2)}) copy-start(bf16[192,128]{1,0:T(8,128)(2,1)} %param.10) | copy-start | bytes 147460
  4.8 42.3 %all-to-all-start = ((bf16[4,128,3072]{2,1,0:T(8,128)(2,1)}), bf16[4,128,3072]{2,1,0:T(8,128)(2,1)S(1)}, u32[]{:S(2)}, u32[]{:S(2)}) async-start(bf16[4,128,3072]{2,1,0:T(8,128)(2,1)} %split_columns.1), calls=%async_computation | async-start | bytes 6291456 | tf_op jit(solution)/shard_map/all_to_all | solution.py:270
  39.3 7.8 %collective-permute-start.1 = (bf16[8,400,128]{2,1,0:T(8,128)(2,1)}, bf16[8,400,128]{2,1,0:T(8,128)(2,1)}, u32[]{:S(2)}, u32[]{:S(2)}) collective-permute-start(bf16[8,400,128]{2,1,0:T(8,128)(2,1)} %bitcast.5.own_ref), channel_id=1, source_target_pairs={{0,4},{4,0},{1,5},{5,1},{2,6},{6,2},{3,7},{7,3},{8,12},{12,8},{9,1... | collective-permute-start | bytes 2457608 | tf_op jit(solution)/shard_map/ppermute | solution.py:254
  49.8 0.8 copy-start
  50.6 13.2 %all-to-all-start.1 = ((f32[4,136,256]{2,1,0:T(8,128)}), f32[4,136,256]{2,1,0:T(8,128)}, u32[]{:S(2)}, u32[]{:S(2)}) async-start(f32[4,136,256]{2,1,0:T(8,128)} %copy-done), calls=%async_computation.1 | async-start | bytes 1114112 | tf_op jit(solution)/shard_map/all_to_all | solution.py:295
  64.8 5.3 %collective-permute-start.2 = (bf16[128,256]{1,0:T(8,128)(2,1)S(1)}, bf16[128,256]{1,0:T(8,128)(2,1)S(1)}, u32[]{:S(2)}, u32[]{:S(2)}) collective-permute-start(bf16[128,256]{1,0:T(8,128)(2,1)S(1)} %slice_reduce_fusion), channel_id=1, source_target_pairs={{0,128},{64,192},{1,129},{65,193},{2,130},{66,194},{3,131},{67,195... | collective-permute-start | bytes 196616 | tf_op jit(solution)/shard_map/ppermute | solution.py:305
  67.4 4.2 %collective-permute-start.3 = (bf16[128,256]{1,0:T(8,128)(2,1)S(1)}, bf16[128,256]{1,0:T(8,128)(2,1)S(1)}, u32[]{:S(2)}, u32[]{:S(2)}) collective-permute-start(bf16[128,256]{1,0:T(8,128)(2,1)S(1)} %slice_reduce_fusion), channel_id=1, source_target_pairs={{0,64},{64,128},{128,192},{1,65},{65,129},{129,193},{2,66},{66,130... | collective-permute-start | bytes 196616 | tf_op jit(solution)/shard_map/ppermute | solution.py:304
  72.7 32.3 %all-to-all-start.2 = ((bf16[8,2,128,256]{3,2,1,0:T(8,128)(2,1)}), bf16[8,2,128,256]{3,2,1,0:T(8,128)(2,1)}, u32[]{:S(2)}, u32[]{:S(2)}) async-start(bf16[8,2,128,256]{3,2,1,0:T(8,128)(2,1)} %pad_maximum_fusion), calls=%async_computation.2 | async-start | bytes 2097152 | tf_op jit(solution)/shard_map/all_to_all | solution.py:314
  79.3 0.7 collective-permute-start
  105.0 10.3 %collective-permute-start.4 = (bf16[8,2,128,256]{3,2,1,0:T(8,128)(2,1)}, bf16[8,2,128,256]{3,2,1,0:T(8,128)(2,1)}, u32[]{:S(2)}, u32[]{:S(2)}) collective-permute-start(bf16[8,2,128,256]{3,2,1,0:T(8,128)(2,1)} %all-to-all-done.2.own), channel_id=1, source_target_pairs={{0,4},{4,0},{1,5},{5,1},{2,6},{6,2},{3,7},{7,3},{8,12},{12,8},{9,1... | collective-permute-start | bytes 3145736 | tf_op jit(solution)/shard_map/ppermute | solution.py:254
  110.0 5.3 %collective-permute-start.5 = (bf16[128,256]{1,0:T(8,128)(2,1)S(1)}, bf16[128,256]{1,0:T(8,128)(2,1)S(1)}, u32[]{:S(2)}, u32[]{:S(2)}) collective-permute-start(bf16[128,256]{1,0:T(8,128)(2,1)S(1)} %collective-permute-done.2.own_back), channel_id=1, source_target_pairs={{0,4},{4,0},{1,5},{5,1},{2,6},{6,2},{3,7},{7,3},{8,12},{12,8},{9,1... | collective-permute-start | bytes 196616 | tf_op jit(solution)/shard_map/ppermute | solution.py:254
  111.0 36.5 %all-to-all-start.3 = ((bf16[8,192,256]{2,1,0:T(8,128)(2,1)}), bf16[8,192,256]{2,1,0:T(8,128)(2,1)}, u32[]{:S(2)}, u32[]{:S(2)}) async-start(bf16[8,192,256]{2,1,0:T(8,128)(2,1)} %broadcast_in_dim.39), calls=%async_computation.3 | async-start | bytes 1572864 | tf_op jit(solution)/shard_map/all_to_all | solution.py:317
  115.3 1.0 copy-start.7
  116.3 1.0 copy-start.8
  117.3 1.0 copy-start.9
  142.8 0.6 copy-start.6
  143.5 2.8 %collective-permute-start.6 = (bf16[8,2,128,256]{3,2,1,0:T(8,128)(2,1)S(1)}, bf16[8,2,128,256]{3,2,1,0:T(8,128)(2,1)S(1)}, u32[]{:S(2)}, u32[]{:S(2)}) collective-permute-start(bf16[8,2,128,256]{3,2,1,0:T(8,128)(2,1)S(1)} %get-tuple-element.44), channel_id=1, source_target_pairs={{0,4},{4,0},{1,5},{5,1},{2,6},{6,2},{3,7},{7,3},{8,12},{12,8},{9,1... | collective-permute-start | bytes 3145736 | tf_op jit(solution)/shard_map/ppermute | solution.py:254
  147.6 36.2 %all-to-all-start.4 = ((bf16[8,2,128,256]{3,2,1,0:T(8,128)(2,1)}), bf16[8,2,128,256]{3,2,1,0:T(8,128)(2,1)}, u32[]{:S(2)}, u32[]{:S(2)}) async-start(bf16[8,2,128,256]{3,2,1,0:T(8,128)(2,1)} %add_convert_fusion), calls=%async_computation.4 | async-start | bytes 2097152 | tf_op jit(solution)/shard_map/all_to_all | solution.py:326
  154.4 19.5 %collective-permute-start.8 = (bf16[8,192,256]{2,1,0:T(8,128)(2,1)}, bf16[8,192,256]{2,1,0:T(8,128)(2,1)}, u32[]{:S(2)}, u32[]{:S(2)}) collective-permute-start(bf16[8,192,256]{2,1,0:T(8,128)(2,1)} %all-to-all-done.3.refs_0_), channel_id=1, source_target_pairs={{0,192},{64,0},{128,64},{192,128},{1,193},{65,1},{129,65},{193,129... | collective-permute-start | bytes 2359304 | tf_op jit(solution)/shard_map/ppermute | solution.py:329
  155.0 19.6 %collective-permute-start.7 = (bf16[8,192,256]{2,1,0:T(8,128)(2,1)}, bf16[8,192,256]{2,1,0:T(8,128)(2,1)}, u32[]{:S(2)}, u32[]{:S(2)}) collective-permute-start(bf16[8,192,256]{2,1,0:T(8,128)(2,1)} %all-to-all-done.3.refs_0_), channel_id=1, source_target_pairs={{0,64},{64,128},{128,192},{192,0},{1,65},{65,129},{129,193},{193,1... | collective-permute-start | bytes 2359304 | tf_op jit(solution)/shard_map/ppermute | solution.py:329
  156.4 31.4 %collective-permute-start.9 = (bf16[128,256]{1,0:T(8,128)(2,1)}, bf16[128,256]{1,0:T(8,128)(2,1)}, u32[]{:S(2)}, u32[]{:S(2)}) collective-permute-start(bf16[128,256]{1,0:T(8,128)(2,1)} %get-tuple-element.49), channel_id=1, source_target_pairs={{0,4},{4,0},{1,5},{5,1},{2,6},{6,2},{3,7},{7,3},{8,12},{12,8},{9,1... | collective-permute-start | bytes 196616 | tf_op jit(solution)/shard_map/ppermute | solution.py:254
  185.8 19.0 %collective-permute-start.11 = (bf16[4,192,256]{2,1,0:T(8,128)(2,1)S(1)}, bf16[4,192,256]{2,1,0:T(8,128)(2,1)S(1)}, u32[]{:S(2)}, u32[]{:S(2)}) collective-permute-start(bf16[4,192,256]{2,1,0:T(8,128)(2,1)S(1)} %slice.41), channel_id=1, source_target_pairs={{0,192},{64,0},{128,64},{192,128},{1,193},{65,1},{129,65},{193,129... | collective-permute-start | bytes 1179656 | tf_op jit(solution)/shard_map/ppermute | solution.py:329
  186.5 18.3 %collective-permute-start.10 = (bf16[4,192,256]{2,1,0:T(8,128)(2,1)S(1)}, bf16[4,192,256]{2,1,0:T(8,128)(2,1)S(1)}, u32[]{:S(2)}, u32[]{:S(2)}) collective-permute-start(bf16[4,192,256]{2,1,0:T(8,128)(2,1)S(1)} %slice.40), channel_id=1, source_target_pairs={{0,64},{64,128},{128,192},{192,0},{1,65},{65,129},{129,193},{193,1... | collective-permute-start | bytes 1179656 | tf_op jit(solution)/shard_map/ppermute | solution.py:329
  204.8 0.7 copy-start.1
  207.2 0.6 copy-start.4
  207.9 6.2 %collective-permute-start.12 = (bf16[8,192,256]{2,1,0:T(8,128)(2,1)S(1)}, bf16[8,192,256]{2,1,0:T(8,128)(2,1)S(1)}, u32[]{:S(2)}, u32[]{:S(2)}) collective-permute-start(bf16[8,192,256]{2,1,0:T(8,128)(2,1)S(1)} %get-tuple-element.54), channel_id=1, source_target_pairs={{0,4},{4,0},{1,5},{5,1},{2,6},{6,2},{3,7},{7,3},{8,12},{12,8},{9,1... | collective-permute-start | bytes 2359304 | tf_op jit(solution)/shard_map/ppermute | solution.py:254
  214.1 6.3 %copy-start.2 = (bf16[4,192,256]{2,1,0:T(8,128)(2,1)S(1)}, bf16[4,192,256]{2,1,0:T(8,128)(2,1)}, u32[]{:S(2)}) copy-start(bf16[4,192,256]{2,1,0:T(8,128)(2,1)} %copy-done.1) | copy-start | bytes 1179652
  214.1 11.3 %copy-start.5 = (bf16[128,256]{1,0:T(8,128)(2,1)S(1)}, bf16[128,256]{1,0:T(8,128)(2,1)}, u32[]{:S(2)}) copy-start(bf16[128,256]{1,0:T(8,128)(2,1)} %copy-done.4) | copy-start | bytes 196612
  215.2 27.9 %all-to-all-start.5 = ((bf16[8,192,256]{2,1,0:T(8,128)(2,1)}), bf16[8,192,256]{2,1,0:T(8,128)(2,1)}, u32[]{:S(2)}, u32[]{:S(2)}) async-start(bf16[8,192,256]{2,1,0:T(8,128)(2,1)} %add_convert_fusion.1), calls=%async_computation.5 | async-start | bytes 1572864 | tf_op jit(solution)/shard_map/all_to_all | solution.py:353
  219.4 4.6 %collective-permute-start.13 = (bf16[8,192,256]{2,1,0:T(8,128)(2,1)}, bf16[8,192,256]{2,1,0:T(8,128)(2,1)S(1)}, u32[]{:S(2)}, u32[]{:S(2)}) collective-permute-start(bf16[8,192,256]{2,1,0:T(8,128)(2,1)} %all-to-all-done.3.refs_0_), channel_id=1, source_target_pairs={{0,4},{4,0},{1,5},{5,1},{2,6},{6,2},{3,7},{7,3},{8,12},{12,8},{9,1... | collective-permute-start | bytes 2359304 | tf_op jit(solution)/shard_map/ppermute | solution.py:254
  219.9 4.4 %collective-permute-start.14 = (bf16[8,192,256]{2,1,0:T(8,128)(2,1)}, bf16[8,192,256]{2,1,0:T(8,128)(2,1)S(1)}, u32[]{:S(2)}, u32[]{:S(2)}) collective-permute-start(bf16[8,192,256]{2,1,0:T(8,128)(2,1)} %collective-permute-done.7.refs_1_), channel_id=1, source_target_pairs={{0,4},{4,0},{1,5},{5,1},{2,6},{6,2},{3,7},{7,3},{8,12},{12,8},{9,1... | collective-permute-start | bytes 2359304 | tf_op jit(solution)/shard_map/ppermute | solution.py:254
  220.0 5.4 %collective-permute-start.17 = (bf16[8,192,256]{2,1,0:T(8,128)(2,1)}, bf16[8,192,256]{2,1,0:T(8,128)(2,1)S(1)}, u32[]{:S(2)}, u32[]{:S(2)}) collective-permute-start(bf16[8,192,256]{2,1,0:T(8,128)(2,1)} %collective-permute-done.8.refs_4_), channel_id=1, source_target_pairs={{0,4},{4,0},{1,5},{5,1},{2,6},{6,2},{3,7},{7,3},{8,12},{12,8},{9,1... | collective-permute-start | bytes 2359304 | tf_op jit(solution)/shard_map/ppermute | solution.py:254
  220.4 2.5 %collective-permute-start.15 = (bf16[4,192,256]{2,1,0:T(8,128)(2,1)S(1)}, bf16[4,192,256]{2,1,0:T(8,128)(2,1)S(1)}, u32[]{:S(2)}, u32[]{:S(2)}) collective-permute-start(bf16[4,192,256]{2,1,0:T(8,128)(2,1)S(1)} %copy-done.2), channel_id=1, source_target_pairs={{0,4},{4,0},{1,5},{5,1},{2,6},{6,2},{3,7},{7,3},{8,12},{12,8},{9,1... | collective-permute-start | bytes 1179656 | tf_op jit(solution)/shard_map/ppermute | solution.py:254
  220.5 3.5 %collective-permute-start.16 = (bf16[4,192,256]{2,1,0:T(8,128)(2,1)S(1)}, bf16[4,192,256]{2,1,0:T(8,128)(2,1)S(1)}, u32[]{:S(2)}, u32[]{:S(2)}) collective-permute-start(bf16[4,192,256]{2,1,0:T(8,128)(2,1)S(1)} %collective-permute-done.11.refs_3_), channel_id=1, source_target_pairs={{0,4},{4,0},{1,5},{5,1},{2,6},{6,2},{3,7},{7,3},{8,12},{12,8},{9,1... | collective-permute-start | bytes 1179656 | tf_op jit(solution)/shard_map/ppermute | solution.py:254
  236.3 1.0 copy-start.3
